TPU v7x, 32 devices: a whole 2x2x4 slice. The times are simulated.
32 devices in a mesh: group: 2 (over x), tensor: 16 (over z, y, core).
Axes of the slice: x: 2, y: 2, z: 4, core: 2. Of those that a mesh axis runs over, the one named last changes fastest.
Arguments:
- tokens: bfloat16 [128, 4096], P(('group', 'tensor')), parts along dimension 0, may hold values from -6 to 6
- cotangent: bfloat16 [128, 4096], P(('group', 'tensor')), parts along dimension 0, may hold values from -6 to 6
- gate_weight: bfloat16 [4096, 16384], P(None, 'tensor'), may hold values from -0.1875 to 0.1875
- up_weight: bfloat16 [4096, 16384], P(None, 'tensor'), may hold values from -0.1875 to 0.1875
- down_weight: bfloat16 [16384, 4096], P('tensor'), may hold values from -0.09375 to 0.09375
- block_mask: int32 [3, 64, 256], P(None, None, 'tensor'), may hold values from 0 to 1, as said below
Outputs:
- mixed: bfloat16 [128, 4096], P(('group', 'tensor')), parts along dimension 0
- input_grad: bfloat16 [128, 4096], P(('group', 'tensor')), parts along dimension 0
- gate_grad: bfloat16 [4096, 32768], P(None, ('group', 'tensor')), parts along dimension 1
- up_grad: bfloat16 [4096, 32768], P(None, ('group', 'tensor')), parts along dimension 1
- down_grad: bfloat16 [32768, 4096], P(('group', 'tensor')), parts along dimension 0
There are 2 independent parts, one for each index of `group`. A program takes and returns all parts, laid end to end along the dimension named above; an argument that names none is the same for every part. Nothing has to cross between parts.
Inputs may be any that keep to these rules, and one draw needn't show every extreme that they name: `block_mask`: each 64 x 64 block is kept (1) or dropped (0); about a quarter are kept, with the share differing from one group of 1024 hidden units to the next.
All inputs are finite; a program needn't handle non-finite values.
Results may differ from a plain program's by a relative error of at most 0.0051.
Values may be sent and summed in bfloat16 or wider, within the bound.
No kernel may reach another device: no remote copies, remote signals or barrier semaphores. Data moves between devices by JAX's collectives and lax.ppermute only.
A program may use at most 128 MiB of HBM per device.

v0:
```python
import jax
import jax.numpy as jnp
from jax import lax
from jax.sharding import PartitionSpec as P


def expand(flags):
    return jnp.repeat(jnp.repeat(flags, 64, axis=0), 64, axis=1)


def shards(tokens, cotangent, gate_weight, up_weight, down_weight, block_mask):
    keep_g = expand(block_mask[0]).astype(jnp.bfloat16)
    keep_u = expand(block_mask[1]).astype(jnp.bfloat16)
    keep_d = expand(block_mask[2]).astype(jnp.bfloat16).T
    gate_masked = gate_weight * keep_g
    up_masked = up_weight * keep_u
    down_masked = down_weight * keep_d
    piece = lax.all_gather(tokens, "tensor", axis=0, tiled=True)
    gate_up = jnp.stack(
        [
            jnp.dot(piece, gate_masked, preferred_element_type=jnp.float32),
            jnp.dot(piece, up_masked, preferred_element_type=jnp.float32),
        ],
        0,
    )
    gate = gate_up[0]
    up = gate_up[1]
    sig = jax.nn.sigmoid(gate)
    act = gate * sig
    hidden = (act * up).astype(jnp.bfloat16)
    mixed = lax.psum_scatter(
        jnp.dot(hidden, down_masked, preferred_element_type=jnp.float32),
        "tensor",
        scatter_dimension=0,
        tiled=True,
    ).astype(jnp.bfloat16)
    all_cotangent = lax.all_gather(cotangent, "tensor", axis=0, tiled=True)
    hidden_grad = jnp.dot(all_cotangent, down_masked.T, preferred_element_type=jnp.float32)
    gate_delta = (hidden_grad * up * sig * (1.0 + gate * (1.0 - sig))).astype(jnp.bfloat16)
    up_delta = (hidden_grad * act).astype(jnp.bfloat16)
    gate_rows = gate_delta
    up_rows = up_delta
    input_grad = lax.psum_scatter(
        jnp.dot(gate_rows, gate_masked.T, preferred_element_type=jnp.float32)
        + jnp.dot(up_rows, up_masked.T, preferred_element_type=jnp.float32),
        "tensor",
        scatter_dimension=0,
        tiled=True,
    ).astype(jnp.bfloat16)
    piece = lax.all_gather(tokens, "tensor", axis=0, tiled=True)
    gate_rows = gate_delta
    up_rows = up_delta
    gate_sum = jnp.dot(piece.T, gate_rows, preferred_element_type=jnp.float32)
    up_sum = jnp.dot(piece.T, up_rows, preferred_element_type=jnp.float32)
    gate_grad = (gate_sum * keep_g.astype(jnp.float32)).astype(jnp.bfloat16)
    up_grad = (up_sum * keep_u.astype(jnp.float32)).astype(jnp.bfloat16)
    down_sum = jnp.dot(hidden.T, all_cotangent, preferred_element_type=jnp.float32)
    down_grad = (down_sum * keep_d.astype(jnp.float32)).astype(jnp.bfloat16)
    return (mixed, input_grad, gate_grad, up_grad, down_grad)


def solution(mesh):
    in_specs = (
        P(("group", "tensor"), None),
        P(("group", "tensor"), None),
        P(None, "tensor"),
        P(None, "tensor"),
        P("tensor", None),
        P(None, None, "tensor"),
    )
    out_specs = (
        P(("group", "tensor"), None),
        P(("group", "tensor"), None),
        P(None, ("group", "tensor")),
        P(None, ("group", "tensor")),
        P(("group", "tensor"), None),
    )
    return jax.shard_map(shards, mesh=mesh, in_specs=in_specs, out_specs=out_specs, check_vma=False)
```

profile of v0, /device:TPU:0, one launch (start us, length us, event | category | flops | bytes accessed | tf_op | source)
XLA Modules:
  0.0 239.9 jit_solution(1746324545931514596)
XLA Ops:
  0.6 0.7 convert.5
  1.4 0.2 broadcast_in_dim.20
  1.6 0.3 convert_element_type.73
  1.9 11.9 %copy.16 = bf16[4096,1024]{0,1:T(8,128)(2,1)} copy(bf16[4096,1024]{1,0:T(8,128)(2,1)} %param.9) | data formatting | bytes 16777216 | tf_op args[3]
  13.8 0.0 copy-start.5
  13.8 7.4 %bitcast_multiply_fusion.3 = bf16[4096,1024]{0,1:T(8,128)(2,1)} fusion(bf16[4096,1024]{0,1:T(8,128)(2,1)} %copy.16, bf16[4096,16]{0,1:T(8,128)(2,1)S(1)} %convert_element_type.73), kind=kLoop, calls=%fused_computation.6 | loop fusion | flops 4194304 | bytes 16908288 | tf_op jit(solution)/shard_map/mul | solution.py:16
  21.2 0.0 copy-done.5
  21.2 24.6 %all-gather = bf16[16,4,4096]{2,1,0:T(4,128)(2,1)S(1)} all-gather(bf16[1,4,4096]{2,1,0:T(4,128)(2,1)S(1)} %bitcast.62), channel_id=1, replica_groups=mesh['group'=2,'tensor'=16] {'tensor'}, dimensions={0}, use_global_device_ids=true | all-gather | bytes 557056 | tf_op jit(solution)/shard_map/all_gather | solution.py:18
  45.7 0.1 reshape.26
  45.9 6.0 %convolution_bitcast_fusion.1 = f32[64,1024]{1,0:T(8,128)S(1)} fusion(bf16[4096,1024]{0,1:T(8,128)(2,1)} %bitcast_multiply_fusion.3, bf16[64,4096]{1,0:T(8,128)(2,1)S(1)} %reshape.26), kind=kOutput, calls=%fused_computation.10 | convolution fusion | flops 536870912 | bytes 9175040 | tf_op jit(solution)/shard_map/dot_general | solution.py:22
  51.9 0.2 broadcast_in_dim.18
  52.1 0.3 convert_element_type.70
  52.4 11.9 %copy.15 = bf16[4096,1024]{0,1:T(8,128)(2,1)} copy(bf16[4096,1024]{1,0:T(8,128)(2,1)} %param.8) | data formatting | bytes 16777216 | tf_op args[2]
  64.3 7.4 %bitcast_multiply_fusion.4 = bf16[4096,1024]{0,1:T(8,128)(2,1)} fusion(bf16[4096,1024]{0,1:T(8,128)(2,1)} %copy.15, bf16[4096,16]{0,1:T(8,128)(2,1)S(1)} %convert_element_type.70), kind=kLoop, calls=%fused_computation.7 | loop fusion | flops 4194304 | bytes 16908288 | tf_op jit(solution)/shard_map/mul | solution.py:15
  71.7 6.0 %convolution_bitcast_fusion.2 = f32[64,1024]{1,0:T(8,128)S(1)} fusion(bf16[4096,1024]{0,1:T(8,128)(2,1)} %bitcast_multiply_fusion.4, bf16[64,4096]{1,0:T(8,128)(2,1)S(1)} %reshape.26), kind=kOutput, calls=%fused_computation.11 | convolution fusion | flops 536870912 | bytes 9175040 | tf_op jit(solution)/shard_map/dot_general | solution.py:21
  77.7 0.2 broadcast_in_dim.22
  77.9 0.3 convert_element_type.77
  78.2 0.0 copy-start.6
  78.2 7.4 %bitcast_multiply_fusion.2 = bf16[1024,4096]{1,0:T(8,128)(2,1)} fusion(bf16[1024,4096]{1,0:T(8,128)(2,1)} %param.10, bf16[4096,16]{0,1:T(8,128)(2,1)S(1)} %convert_element_type.77), kind=kLoop, calls=%fused_computation.5 | loop fusion | flops 4194304 | bytes 16908288 | tf_op jit(solution)/shard_map/mul | solution.py:17
  85.6 0.0 copy-done.6
  85.6 19.0 %all-gather.1 = bf16[16,4,4096]{2,1,0:T(4,128)(2,1)S(1)} all-gather(bf16[1,4,4096]{2,1,0:T(4,128)(2,1)S(1)} %bitcast.63), channel_id=1, replica_groups=mesh['group'=2,'tensor'=16] {'tensor'}, dimensions={0}, use_global_device_ids=true | all-gather | bytes 557056 | tf_op jit(solution)/shard_map/all_gather | solution.py:37
  104.7 0.1 reshape.28
  104.8 6.1 %multiply_convert_fusion.1 = (bf16[64,1024]{1,0:T(8,128)(2,1)S(1)}, bf16[64,1024]{1,0:T(8,128)(2,1)S(1)}, bf16[64,1024]{1,0:T(8,128)(2,1)S(1)}) fusion(f32[64,1024]{1,0:T(8,128)S(1)} %convolution_bitcast_fusion.2, f32[64,1024]{1,0:T(8,128)S(1)} %convolution_bitcast_fusion.1, bf16[1024,4096]{1,0:T(8,128)(2,1)} %bitcast_multiply_fusion.2, ...), kind=kOutput, calls=%fused_computation.12 | convolution fusion | flops 537853952 | bytes 9830400 | tf_op jit(solution)/shard_map/dot_general | solution.py:38
  110.9 0.0 copy-start.2
  110.9 0.0 copy-start.4
  110.9 0.0 copy-start
  110.9 0.0 slice-start
  110.9 0.0 slice-start.1
  110.9 0.0 slice-start.2
  110.9 5.1 %fusion.4 = f32[64,4096]{1,0:T(8,128)S(1)} fusion(bf16[64,1024]{1,0:T(8,128)(2,1)S(1)} %get-tuple-element.18, bf16[4096,1024]{0,1:T(8,128)(2,1)} %bitcast_multiply_fusion.4), kind=kOutput, calls=%fused_computation.23 | convolution fusion | flops 536870912 | bytes 9568256 | tf_op jit(solution)/shard_map/dot_general | solution.py:44
  116.0 0.0 slice-done
  116.1 0.8 slice-done.1
  116.9 0.0 slice-start.3
  116.9 1.6 convolution_add_fusion
  118.5 0.0 copy-done.2
  118.5 0.0 copy-done.4
  118.5 0.0 copy-done
  118.5 0.0 slice-done.2
  118.5 1.0 slice-done.3
  119.5 0.0 copy-start.7
  119.5 1.6 fusion.3
  121.1 73.9 %all-reduce.4 = (bf16[64,4096]{1,0:T(8,128)(2,1)}, bf16[64,4096]{1,0:T(8,128)(2,1)}) all-reduce(f32[64,4096]{1,0:T(8,128)S(1)} %fusion.3, f32[64,4096]{1,0:T(8,128)S(1)} %convolution_add_fusion), channel_id=2, replica_groups=mesh['group'=2,'tensor'=16] {'tensor'}, use_global_device_ids=true, to_apply=%region_0.0.clone | all-reduce | flops 524288 | bytes 3145728
  195.0 0.0 copy-done.7
  195.0 0.6 dynamic-slice
  196.2 1.5 dynamic-slice_convert_fusion
  197.7 6.7 %fusion.1 = bf16[4096,1024]{0,1:T(8,128)(2,1)} fusion(bf16[64,1024]{1,0:T(8,128)(2,1)} %copy-done.4, bf16[64,4096]{1,0:T(8,128)(2,1)S(1)} %reshape.26, bf16[4096,16]{0,1:T(8,128)(2,1)S(1)} %convert_element_type.70), kind=kOutput, calls=%fused_computation.3 | convolution fusion | flops 549453824 | bytes 9175040 | tf_op jit(solution)/shard_map/dot_general | solution.py:53
  204.4 0.0 copy-start.3
  204.4 12.0 %copy.17 = bf16[4096,1024]{1,0:T(8,128)(2,1)} copy(bf16[4096,1024]{0,1:T(8,128)(2,1)} %fusion.1) | data formatting | bytes 16777216
  216.4 0.0 copy-done.3
  216.4 5.8 %fusion = bf16[4096,1024]{0,1:T(8,128)(2,1)} fusion(bf16[64,1024]{1,0:T(8,128)(2,1)S(1)} %copy-done.3, bf16[64,4096]{1,0:T(8,128)(2,1)S(1)} %reshape.26, bf16[4096,16]{0,1:T(8,128)(2,1)S(1)} %convert_element_type.73), kind=kOutput, calls=%fused_computation.1 | convolution fusion | flops 549453824 | bytes 9175040 | tf_op jit(solution)/shard_map/dot_general | solution.py:54
  222.2 0.0 copy-start.1
  222.2 12.0 %copy.18 = bf16[4096,1024]{1,0:T(8,128)(2,1)} copy(bf16[4096,1024]{0,1:T(8,128)(2,1)} %fusion) | data formatting | bytes 16777216
  234.1 0.0 copy-done.1
  234.1 5.8 %multiply_convert_fusion = bf16[1024,4096]{1,0:T(8,128)(2,1)} fusion(bf16[64,1024]{1,0:T(8,128)(2,1)S(1)} %copy-done.1, bf16[64,4096]{1,0:T(8,128)(2,1)S(1)} %reshape.28, bf16[4096,16]{0,1:T(8,128)(2,1)S(1)} %convert_element_type.77), kind=kOutput, calls=%fused_computation.4 | convolution fusion | flops 549453824 | bytes 9175040 | tf_op jit(solution)/shard_map/dot_general | solution.py:57
  (3 shorter events, 0.0 us)
Async XLA Ops:
  13.8 7.4 %copy-start.5 = (bf16[4,4096]{1,0:T(4,128)(2,1)S(1)}, bf16[4,4096]{1,0:T(4,128)(2,1)}, u32[]{:S(2)}) copy-start(bf16[4,4096]{1,0:T(4,128)(2,1)} %param.6) | copy-start | bytes 98308
  78.2 7.4 %copy-start.6 = (bf16[4,4096]{1,0:T(4,128)(2,1)S(1)}, bf16[4,4096]{1,0:T(4,128)(2,1)}, u32[]{:S(2)}) copy-start(bf16[4,4096]{1,0:T(4,128)(2,1)} %param.7) | copy-start | bytes 98308
  110.9 7.6 %copy-start.2 = (bf16[64,1024]{1,0:T(8,128)(2,1)}, bf16[64,1024]{1,0:T(8,128)(2,1)S(1)}, u32[]{:S(2)}) copy-start(bf16[64,1024]{1,0:T(8,128)(2,1)S(1)} %get-tuple-element.17) | copy-start | bytes 393220
  110.9 7.6 %copy-start.4 = (bf16[64,1024]{1,0:T(8,128)(2,1)}, bf16[64,1024]{1,0:T(8,128)(2,1)S(1)}, u32[]{:S(2)}) copy-start(bf16[64,1024]{1,0:T(8,128)(2,1)S(1)} %get-tuple-element.18) | copy-start | bytes 393220
  110.9 7.6 %copy-start = (bf16[64,1024]{1,0:T(8,128)(2,1)}, bf16[64,1024]{1,0:T(8,128)(2,1)S(1)}, u32[]{:S(2)}) copy-start(bf16[64,1024]{1,0:T(8,128)(2,1)S(1)} %get-tuple-element.19) | copy-start | bytes 393220
  110.9 5.1 %slice-start = ((s8[8388608]{0:T(1024)(128)(4,1)}), s8[4194304]{0:T(1024)(128)(4,1)S(1)}, s32[]{:S(2)}) async-start(s8[8388608]{0:T(1024)(128)(4,1)} %bitcast.58), calls=%async_computation | async-start | bytes 8388608
  110.9 6.0 %slice-start.1 = ((s8[8388608]{0:T(1024)(128)(4,1)}), s8[4194304]{0:T(1024)(128)(4,1)S(1)}, s32[]{:S(2)}) async-start(s8[8388608]{0:T(1024)(128)(4,1)} %bitcast.58), calls=%async_computation.1 | async-start | bytes 8388608
  110.9 7.6 %slice-start.2 = ((s8[8388608]{0:T(1024)(128)(4,1)}), s8[4194304]{0:T(1024)(128)(4,1)S(1)}, s32[]{:S(2)}) async-start(s8[8388608]{0:T(1024)(128)(4,1)} %bitcast.60), calls=%async_computation.2 | async-start | bytes 8388608
  116.9 2.6 %slice-start.3 = ((s8[8388608]{0:T(1024)(128)(4,1)}), s8[4194304]{0:T(1024)(128)(4,1)S(1)}, s32[]{:S(2)}) async-start(s8[8388608]{0:T(1024)(128)(4,1)} %bitcast.60), calls=%async_computation.3 | async-start | bytes 8388608
  119.5 75.5 %copy-start.7 = (u32[32]{0:T(128)S(1)}, u32[32]{0:T(128)}, u32[]{:S(2)}) copy-start(u32[32]{0:T(128)} %constant.6) | copy-start | bytes 388
  204.4 12.0 %copy-start.3 = (bf16[64,1024]{1,0:T(8,128)(2,1)S(1)}, bf16[64,1024]{1,0:T(8,128)(2,1)}, u32[]{:S(2)}) copy-start(bf16[64,1024]{1,0:T(8,128)(2,1)} %copy-done.2) | copy-start | bytes 393220
  222.2 12.0 %copy-start.1 = (bf16[64,1024]{1,0:T(8,128)(2,1)S(1)}, bf16[64,1024]{1,0:T(8,128)(2,1)}, u32[]{:S(2)}) copy-start(bf16[64,1024]{1,0:T(8,128)(2,1)} %copy-done) | copy-start | bytes 393220
where the time goes:
time: 241 us; the launch traced here: 240 us
  blocking collectives  117 us (49%)
  local copies, waits for them, and re-layouts  53.4 us (22%)
  matrix products  44.6 us (19%)
  other arithmetic  22.9 us (10%)
    unnamed x1, blocking collectives  73.9 us
    unnamed x31, local copies, waits for them, and re-layouts  50.5 us
    all_gather x1, blocking collectives, shards(): piece = lax.all_gather(tokens, 'tensor', axis=0, tiled=True)  24.6 us
    all_gather x1, blocking collectives, shards(): all_cotangent = lax.all_gather(cotangent, 'tensor', axis=0, tiled=True)  19 us
    mul x1, other arithmetic, shards(): down_masked = down_weight * keep_d  7.41 us
    mul x1, other arithmetic, shards(): up_masked = up_weight * keep_u  7.4 us
    mul x1, other arithmetic, shards(): gate_masked = gate_weight * keep_g  7.39 us
    dot_general x1, matrix products, shards(): gate_sum = jnp.dot(piece.T, gate_rows, preferred_element_type=jnp.float32)  6.67 us

commit v1 on v0

v1 whole, which is shorter than its diff:
```python
import functools

import jax
import jax.numpy as jnp
from jax import lax
from jax.experimental import pallas as pl
from jax.experimental.pallas import tpu as pltpu
from jax.sharding import PartitionSpec as P

AXIS = "tensor"
BLOCK = 64
BF16 = jnp.bfloat16
F32 = jnp.float32
MIB = 2**20
VMEM = pl.BlockSpec(memory_space=pltpu.VMEM)


def dot(a, b, ca=1, cb=0):
    return lax.dot_general(a, b, (((ca,), (cb,)), ((), ())), preferred_element_type=F32)


def in_vmem(x):
    return pltpu.with_memory_space_constraint(x, pltpu.VMEM)


def shape(*dims, dtype=F32):
    return jax.ShapeDtypeStruct(dims, dtype)


def params(mib):
    return pltpu.CompilerParams(vmem_limit_bytes=mib * MIB)


def cost(flops, size):
    return pl.CostEstimate(flops=flops, bytes_accessed=size, transcendentals=0)


def spread(blocks, wide):
    row = lax.broadcasted_iota(jnp.int32, (blocks, wide), 0)
    column = lax.broadcasted_iota(jnp.int32, (blocks, wide), 1)
    return (row == column // BLOCK).astype(BF16)


def mask_kernel(transposed, flags_ref, weight_ref, masked_ref, keep_ref):
    rows, columns = weight_ref.shape
    flags = flags_ref[...].astype(F32).astype(BF16)
    keep = dot(flags, spread(columns // BLOCK, columns), 0 if transposed else 1, 0)
    keep_ref[...] = keep
    keep = keep.astype(BF16)
    for block in range(rows // BLOCK):
        at = pl.ds(block * BLOCK, BLOCK)
        masked_ref[at, :] = weight_ref[at, :] * keep[block : block + 1, :]


def mask_weight(flags, weight, transposed):
    rows, columns = weight.shape
    return pl.pallas_call(
        functools.partial(mask_kernel, transposed),
        out_shape=(
            pltpu.VMEM((rows, columns), BF16),
            shape(rows // BLOCK, columns),
        ),
        in_specs=[VMEM, VMEM],
        out_specs=(VMEM, VMEM),
        input_output_aliases={1: 0},
        compiler_params=params(12),
        cost_estimate=cost(0, rows * columns),
        name="mask",
    )(flags, in_vmem(weight))


def forward_kernel(pieces, *refs):
    tokens = refs[:pieces]
    gate_ref, up_ref, down_ref = refs[pieces : pieces + 3]
    all_ref, act_ref, slope_ref, hidden_ref, hidden_t_ref, mine_ref, theirs_ref = refs[pieces + 3 :]
    all_ref[...] = jnp.concatenate([piece[...] for piece in tokens], 0)
    units = gate_ref.shape[1]
    for start in range(0, units, 256):
        at = pl.ds(start, 256)
        gate = dot(all_ref[...], gate_ref[:, at])
        up = dot(all_ref[...], up_ref[:, at])
        sig = jax.nn.sigmoid(gate)
        act = gate * sig
        act_ref[:, at] = act
        slope_ref[:, at] = up * sig * (1.0 + gate * (1.0 - sig))
        hidden = act * up
        hidden_ref[:, at] = hidden.astype(BF16)
        hidden_t_ref[at, :] = hidden.T.astype(BF16)
    half = all_ref.shape[0] // 2
    for start in range(0, down_ref.shape[1], 512):
        at = pl.ds(start, 512)
        mixed = dot(hidden_ref[...], down_ref[:, at])
        mine_ref[:, at] = mixed[:half]
        theirs_ref[:, at] = mixed[half:].astype(BF16)


def forward(tokens, gate, up, down):
    rows = sum(piece.shape[0] for piece in tokens)
    features, units = gate.shape
    return pl.pallas_call(
        functools.partial(forward_kernel, len(tokens)),
        out_shape=(
            shape(rows, features, dtype=BF16),
            shape(rows, units),
            shape(rows, units),
            shape(rows, units, dtype=BF16),
            shape(units, rows, dtype=BF16),
            shape(rows // 2, features),
            shape(rows // 2, features, dtype=BF16),
        ),
        in_specs=[VMEM] * (len(tokens) + 3),
        out_specs=(VMEM,) * 7,
        compiler_params=params(16),
        cost_estimate=cost(6 * rows * features * units, 3 * 2 * features * units),
        name="forward",
    )(*tokens, *map(in_vmem, (gate, up, down)))


def backward_kernel(pieces, *refs):
    cotangents = refs[:pieces]
    act_ref, slope_ref, gate_ref, up_ref, down_ref = refs[pieces : pieces + 5]
    all_ref, gate_delta_ref, up_delta_ref, mine_ref, theirs_ref = refs[pieces + 5 :]
    all_ref[...] = jnp.concatenate([piece[...] for piece in cotangents], 0)
    features, units = gate_ref.shape
    for start in range(0, units, 256):
        at = pl.ds(start, 256)
        hidden_grad = dot(all_ref[...], down_ref[at, :], 1, 1)
        gate_delta_ref[:, at] = (hidden_grad * slope_ref[:, at]).astype(BF16)
        up_delta_ref[:, at] = (hidden_grad * act_ref[:, at]).astype(BF16)
    half = all_ref.shape[0] // 2
    for start in range(0, features, 512):
        at = pl.ds(start, 512)
        grad = dot(gate_delta_ref[...], gate_ref[at, :], 1, 1)
        grad += dot(up_delta_ref[...], up_ref[at, :], 1, 1)
        mine_ref[:, at] = grad[:half]
        theirs_ref[:, at] = grad[half:].astype(BF16)


def backward(cotangents, act, slope, gate, up, down):
    rows = sum(piece.shape[0] for piece in cotangents)
    features, units = gate.shape
    return pl.pallas_call(
        functools.partial(backward_kernel, len(cotangents)),
        out_shape=(
            shape(rows, features, dtype=BF16),
            shape(rows, units, dtype=BF16),
            shape(rows, units, dtype=BF16),
            shape(rows // 2, features),
            shape(rows // 2, features, dtype=BF16),
        ),
        in_specs=[VMEM] * (len(cotangents) + 5),
        out_specs=(VMEM,) * 5,
        compiler_params=params(16),
        cost_estimate=cost(6 * rows * features * units, 3 * 2 * features * units),
        name="backward",
    )(*cotangents, act, slope, *map(in_vmem, (gate, up, down)))


def grads_kernel(
    tokens_ref, cotangent_ref, gate_delta_ref, up_delta_ref, hidden_t_ref, keep_g_ref, keep_u_ref, keep_d_ref,
    gate_ref, up_ref, down_ref,
):
    step = pl.program_id(0)
    blocks = gate_ref.shape[0] // BLOCK
    for delta_ref, keep_ref, out_ref in (
        (gate_delta_ref, keep_g_ref, gate_ref),
        (up_delta_ref, keep_u_ref, up_ref),
    ):
        grad = dot(tokens_ref[...], delta_ref[...], 0, 0)
        for block in range(blocks):
            keep = keep_ref[pl.ds(step * blocks + block, 1), :]
            at = slice(block * BLOCK, (block + 1) * BLOCK)
            out_ref[at, :] = (grad[at, :] * keep).astype(BF16)
    grad = dot(hidden_t_ref[...], cotangent_ref[...])
    down_ref[...] = (grad * keep_d_ref[pl.ds(step, 1), :]).astype(BF16)


def grads(tokens, cotangents, gate_delta, up_delta, hidden_t, keeps):
    rows, features = tokens.shape
    units = hidden_t.shape[0]
    steps = units // BLOCK
    wide = features // steps
    return pl.pallas_call(
        grads_kernel,
        grid=(steps,),
        out_shape=(
            shape(features, units, dtype=BF16),
            shape(features, units, dtype=BF16),
            shape(units, features, dtype=BF16),
        ),
        in_specs=[
            pl.BlockSpec((rows, wide), lambda i: (0, i)),
            VMEM,
            VMEM,
            VMEM,
            pl.BlockSpec((BLOCK, rows), lambda i: (i, 0)),
            VMEM,
            VMEM,
            VMEM,
        ],
        out_specs=(
            pl.BlockSpec((wide, units), lambda i: (i, 0)),
            pl.BlockSpec((wide, units), lambda i: (i, 0)),
            pl.BlockSpec((BLOCK, features), lambda i: (i, 0)),
        ),
        compiler_params=params(16),
        cost_estimate=cost(6 * rows * features * units, 3 * 2 * features * units),
        name="grads",
    )(tokens, cotangents, gate_delta, up_delta, hidden_t, *keeps)


def across_cores(devices):
    return [(i, i ^ 1) for i in range(devices)]


def across_chips(devices):
    def pairs(offsets):
        return [(i, ((i // 2) ^ offsets[i % 2]) * 2 + i % 2) for i in range(devices)]

    return [pairs((k + 1, k) if k else (0, 1)) for k in range(0, devices // 2, 2)]


def gather(x, devices):
    own = jnp.concatenate([x, lax.ppermute(x, AXIS, across_cores(devices))], 0)
    mine = [lax.ppermute(own, AXIS, pairs) for pairs in across_chips(devices)]
    return mine + [lax.ppermute(piece, AXIS, across_cores(devices)) for piece in mine]


def scatter(mine, theirs, devices):
    total = (mine + lax.ppermute(theirs, AXIS, across_cores(devices)).astype(F32)).astype(BF16)
    chips = across_chips(devices)
    rows = total.shape[0] // len(chips)
    parts = [lax.ppermute(total[k * rows : (k + 1) * rows], AXIS, pairs) for k, pairs in enumerate(chips)]
    part = sum(p.astype(F32) for p in parts)
    half = rows // 2
    return (part[:half] + lax.ppermute(part[half:], AXIS, across_cores(devices))).astype(BF16)


def shards(devices, tokens, cotangent, gate_weight, up_weight, down_weight, block_mask):
    gate, keep_g = mask_weight(block_mask[0], gate_weight, False)
    up, keep_u = mask_weight(block_mask[1], up_weight, False)
    down, keep_d = mask_weight(block_mask[2], down_weight, True)
    token_pieces = gather(tokens, devices)
    cotangent_pieces = gather(cotangent, devices)
    all_tokens, act, slope, _, hidden_t, mixed_mine, mixed_theirs = forward(token_pieces, gate, up, down)
    mixed = scatter(mixed_mine, mixed_theirs, devices)
    all_cotangents, gate_delta, up_delta, grad_mine, grad_theirs = backward(
        cotangent_pieces, act, slope, gate, up, down
    )
    input_grad = scatter(grad_mine, grad_theirs, devices)
    gate_grad, up_grad, down_grad = grads(
        all_tokens, all_cotangents, gate_delta, up_delta, hidden_t, (keep_g, keep_u, keep_d)
    )
    return mixed, input_grad, gate_grad, up_grad, down_grad


def solution(mesh):
    in_specs = (
        P(("group", AXIS), None),
        P(("group", AXIS), None),
        P(None, AXIS),
        P(None, AXIS),
        P(AXIS, None),
        P(None, None, AXIS),
    )
    out_specs = (
        P(("group", AXIS), None),
        P(("group", AXIS), None),
        P(None, ("group", AXIS)),
        P(None, ("group", AXIS)),
        P(("group", AXIS), None),
    )
    body = functools.partial(shards, mesh.shape[AXIS])
    return jax.shard_map(body, mesh=mesh, in_specs=in_specs, out_specs=out_specs, check_vma=False)
```

time: 241 us -> 110 us (0.46)
  blocking collectives: 117 us -> 0 us
  matrix products: 44.6 us -> 0 us
  starting transfers between devices: 0 us -> 32.7 us
  Pallas kernels: 0 us -> 29.7 us
  other arithmetic: 22.9 us -> 1.5 us
  local copies, waits for them, and re-layouts: 53.4 us -> 35.7 us
  waiting for transfers between devices: 0 us -> 9.04 us
    unnamed x1 -> x0, blocking collectives: 73.9 us -> none
    dot_general x9 -> x0, matrix products: 44.6 us -> none  [the longest x1 6.67 us: shards(): gate_sum = jnp.dot(piece.T, gate_rows, preferred_element_type=jnp.float32)]
    all_gather x2 -> x0, blocking collectives: 43.6 us -> none  [the longest x1 24.6 us: shards(): piece = lax.all_gather(tokens, 'tensor', axis=0, tiled=True)]
    ppermute x0 -> x30, starting transfers between devices: none -> 32.7 us  [the longest x8 14.3 us: gather(): mine = [lax.ppermute(own, AXIS, pairs) for pairs in across_chips(devices)]]
    pallas_call x0 -> x6, Pallas kernels: none -> 29.7 us  [the longest x1 12.5 us: grads(): pl.pallas_call(grads_kernel, grid=(steps,), out_shape=(shape(features, un...]
    mul x3 -> x0, other arithmetic: 22.2 us -> none  [the longest x1 7.41 us: shards(): down_masked = down_weight * keep_d]
    unnamed x31 -> x24, local copies, waits for them, and re-layouts: 50.5 us -> 35.6 us
    ppermute x0 -> x30, waiting for transfers between devices: none -> 9.04 us  [the longest x8 5.5 us: scatter(): lax.ppermute(total[k * rows:(k + 1) * rows], AXIS, pairs)]
  transfers between devices with their start and end apart: 0 -> 30, of which waited for: 0 -> 5; matrix products, arithmetic and copies ran while one was open for 0% -> 1% of each run, Pallas kernels for 0% -> 20%
where the time goes in v1:
time: 110 us
  local copies, waits for them, and re-layouts  35.7 us (32%)
  starting transfers between devices  32.7 us (30%)
  Pallas kernels  29.7 us (27%)
  waiting for transfers between devices  9.04 us (8%)
  other arithmetic  1.5 us (1%)
    unnamed x24, local copies, waits for them, and re-layouts  35.6 us
    ppermute x8, starting transfers between devices, gather(): mine = [lax.ppermute(own, AXIS, pairs) for pairs in across_chips(devices)]  14.3 us
    ppermute x8, starting transfers between devices, scatter(): lax.ppermute(total[k * rows:(k + 1) * rows], AXIS, pairs)  12.9 us
    pallas_call x1, Pallas kernels, grads(): pl.pallas_call(grads_kernel, grid=(steps,), out_shape=(shape(features, un...  12.5 us
    pallas_call x1, Pallas kernels, backward(): pl.pallas_call(functools.partial(backward_kernel, len(cotangents)), out_s...  7.93 us
    ppermute x8, waiting for transfers between devices, scatter(): lax.ppermute(total[k * rows:(k + 1) * rows], AXIS, pairs)  5.5 us
    pallas_call x3, Pallas kernels, mask_weight(): pl.pallas_call(functools.partial(mask_kernel, transposed), out_shape=(plt...  4.83 us
    pallas_call x1, Pallas kernels, forward(): pl.pallas_call(functools.partial(forward_kernel, len(tokens)), out_shape=...  4.53 us
  transfers between devices with their start and end apart: 30, of which 5 were waited for; matrix products, arithmetic and copies ran while one was open for 1% of the time, Pallas kernels for 20%

profile of v1, /device:TPU:0, one launch (start us, length us, event | category | flops | bytes accessed | tf_op | source)
XLA Modules:
  0.0 109.6 jit_solution(18262247965725279485)
XLA Ops:
  0.6 7.8 %copy.26.weight_ref = bf16[4096,1024]{1,0:T(8,128)(2,1)} copy(bf16[4096,1024]{1,0:T(8,128)(2,1)} %param.8) | data formatting | bytes 16777216
  8.4 7.8 %copy.27.weight_ref = bf16[4096,1024]{1,0:T(8,128)(2,1)} copy(bf16[4096,1024]{1,0:T(8,128)(2,1)} %param.9) | data formatting | bytes 16777216
  16.2 7.9 %copy.28.weight_ref = bf16[1024,4096]{1,0:T(8,128)(2,1)} copy(bf16[1024,4096]{1,0:T(8,128)(2,1)} %param.10) | data formatting | bytes 16777216
  24.1 0.5 collective-permute-start
  24.5 0.1 collective-permute-start.15
  24.6 0.8 collective-permute-done
  25.4 0.7 collective-permute-start.1
  26.1 3.9 %collective-permute-start.2 = (bf16[8,4096]{1,0:T(8,128)(2,1)S(1)}, bf16[8,4096]{1,0:T(8,128)(2,1)S(1)}, u32[]{:S(2)}, u32[]{:S(2)}) collective-permute-start(bf16[8,4096]{1,0:T(8,128)(2,1)S(1)} %pad_maximum_fusion), channel_id=1, source_target_pairs={{0,6},{1,5},{2,4},{3,7},{4,2},{5,1},{6,0},{7,3},{8,14},{9,13},{10,... | collective-permute-start | bytes 196616 | tf_op jit(solution)/shard_map/ppermute | solution.py:225
  30.0 2.5 %collective-permute-start.3 = (bf16[8,4096]{1,0:T(8,128)(2,1)S(1)}, bf16[8,4096]{1,0:T(8,128)(2,1)S(1)}, u32[]{:S(2)}, u32[]{:S(2)}) collective-permute-start(bf16[8,4096]{1,0:T(8,128)(2,1)S(1)} %pad_maximum_fusion), channel_id=1, source_target_pairs={{0,10},{1,9},{2,8},{3,11},{4,14},{5,13},{6,12},{7,15},{8,2},{9,1},... | collective-permute-start | bytes 196616 | tf_op jit(solution)/shard_map/ppermute | solution.py:225
  32.5 1.2 %collective-permute-start.4 = (bf16[8,4096]{1,0:T(8,128)(2,1)S(1)}, bf16[8,4096]{1,0:T(8,128)(2,1)S(1)}, u32[]{:S(2)}, u32[]{:S(2)}) collective-permute-start(bf16[8,4096]{1,0:T(8,128)(2,1)S(1)} %pad_maximum_fusion), channel_id=1, source_target_pairs={{0,14},{1,13},{2,12},{3,15},{4,10},{5,9},{6,8},{7,11},{8,6},{9,5},... | collective-permute-start | bytes 196616 | tf_op jit(solution)/shard_map/ppermute | solution.py:225
  33.7 0.0 collective-permute-done.15
  33.8 0.8 collective-permute-start.16
  34.6 0.0 collective-permute-done.1.refs_0_
  34.6 0.7 collective-permute-start.17
  35.3 4.4 %collective-permute-start.18 = (bf16[8,4096]{1,0:T(8,128)(2,1)S(1)}, bf16[8,4096]{1,0:T(8,128)(2,1)S(1)}, u32[]{:S(2)}, u32[]{:S(2)}) collective-permute-start(bf16[8,4096]{1,0:T(8,128)(2,1)S(1)} %pad_maximum_fusion.1), channel_id=1, source_target_pairs={{0,10},{1,9},{2,8},{3,11},{4,14},{5,13},{6,12},{7,15},{8,2},{9,1},... | collective-permute-start | bytes 196616 | tf_op jit(solution)/shard_map/ppermute | solution.py:225
  39.8 0.0 collective-permute-done.3.refs_2_
  39.8 0.0 collective-permute-start.19
  39.8 0.0 collective-permute-done.4.refs_3_
  39.8 1.6 %collective-permute-start.5 = (bf16[8,4096]{1,0:T(8,128)(2,1)S(1)}, bf16[8,4096]{1,0:T(8,128)(2,1)S(1)}, u32[]{:S(2)}, u32[]{:S(2)}) collective-permute-start(bf16[8,4096]{1,0:T(8,128)(2,1)S(1)} %collective-permute-done.1.refs_0_), channel_id=1, source_target_pairs={{0,1},{1,0},{2,3},{3,2},{4,5},{5,4},{6,7},{7,6},{8,9},{9,8},{10,11... | collective-permute-start | bytes 196616 | tf_op jit(solution)/shard_map/ppermute | solution.py:226
  41.4 0.1 collective-permute-start.6
  41.4 0.4 collective-permute-start.7
  41.9 2.1 %collective-permute-done.18.refs_2_ = bf16[8,4096]{1,0:T(8,128)(2,1)S(1)} collective-permute-done((bf16[8,4096]{1,0:T(8,128)(2,1)S(1)}, bf16[8,4096]{1,0:T(8,128)(2,1)S(1)}, u32[]{:S(2)}, u32[]{:S(2)}) %collective-permute-start.18) | collective-permute-done | bytes 65568 | tf_op jit(solution)/shard_map/ppermute | solution.py:225
  44.0 0.0 collective-permute-start.8
  44.0 0.1 copy.17
  44.1 0.1 copy.18
  44.2 0.1 copy.19
  44.2 0.0 copy-start.1
  44.3 3.5 %copy-done.1 = bf16[4096,1024]{1,0:T(8,128)(2,1)S(1)} copy-done((bf16[4096,1024]{1,0:T(8,128)(2,1)S(1)}, bf16[4096,1024]{1,0:T(8,128)(2,1)}, u32[]{:S(2)}) %copy-start.1) | copy-done | bytes 8388632
  47.8 1.3 %mask.3 = (bf16[4096,1024]{1,0:T(8,128)(2,1)S(1)}, f32[64,1024]{1,0:T(8,128)S(1)}) custom-call(s32[64,16]{1,0:T(8,128)S(1)} %bitcast.7, bf16[4096,1024]{1,0:T(8,128)(2,1)S(1)} %copy-done.1), custom_call_target="tpu_custom_call", output_to_operand_aliasing={{0}: (1, {})} | custom-call | bytes 4194304 | tf_op jit(solution)/shard_map/mask/pallas_call | solution.py:57
  49.1 0.0 copy-start.2
  49.1 0.9 copy-done
  50.0 1.3 %mask.4 = (bf16[4096,1024]{1,0:T(8,128)(2,1)S(1)}, f32[64,1024]{1,0:T(8,128)S(1)}) custom-call(s32[64,16]{1,0:T(8,128)S(1)} %bitcast.6, bf16[4096,1024]{1,0:T(8,128)(2,1)S(1)} %copy-done), custom_call_target="tpu_custom_call", output_to_operand_aliasing={{0}: (1, {})} | custom-call | bytes 4194304 | tf_op jit(solution)/shard_map/mask/pallas_call | solution.py:57
  51.3 2.9 %slice-done = s8[4194304]{0:T(1024)(128)(4,1)S(1)} async-done(((s8[8388608]{0:T(1024)(128)(4,1)}), s8[4194304]{0:T(1024)(128)(4,1)S(1)}, s32[]{:S(2)}) %slice-start) | async-done | bytes 4194328
  54.2 1.2 %slice-done.1 = s8[4194304]{0:T(1024)(128)(4,1)S(1)} async-done(((s8[8388608]{0:T(1024)(128)(4,1)}), s8[4194304]{0:T(1024)(128)(4,1)S(1)}, s32[]{:S(2)}) %slice-start.1) | async-done | bytes 4194328
  55.4 2.3 %mask.5 = (bf16[1024,4096]{1,0:T(8,128)(2,1)S(1)}, f32[16,4096]{1,0:T(8,128)S(1)}) custom-call(s32[64,16]{1,0:T(8,128)S(1)} %bitcast.5, bf16[1024,4096]{1,0:T(8,128)(2,1)S(1)} %bitcast.4), custom_call_target="tpu_custom_call", output_to_operand_aliasing={{0}: (1, {})} | custom-call | bytes 4194304 | tf_op jit(solution)/shard_map/mask/pallas_call | solution.py:57
  57.7 0.6 collective-permute-start.20
  58.3 0.0 collective-permute-done.5.refs_4_
  58.3 0.1 collective-permute-start.21
  58.4 0.4 collective-permute-start.22
  58.8 0.0 collective-permute-done.7.refs_6_
  58.8 0.1 collective-permute-start.23
  58.9 3.4 %copy-done.3 = bf16[4096,1024]{1,0:T(8,128)(2,1)S(1)} copy-done((bf16[4096,1024]{1,0:T(8,128)(2,1)S(1)}, bf16[4096,1024]{1,0:T(8,128)(2,1)}, u32[]{:S(2)}) %copy-start.3) | copy-done | bytes 8388632
  62.3 4.5 %forward.1 = (bf16[64,4096]{1,0:T(8,128)(2,1)S(1)}, f32[64,1024]{1,0:T(8,128)S(1)}, f32[64,1024]{1,0:T(8,128)S(1)}, bf16[64,1024]{1,0:T(8,128)(2,1)}, bf16[1024,...) custom-call(bf16[8,4096]{1,0:T(8,128)(2,1)S(1)} %collective-permute-done.1.refs_0_, ...), custom_call_target="tpu_custom_call" | custom-call | flops 1610612736 | bytes 25165824 | tf_op jit(solution)/shard_map/forward/pallas_call | solution.py:100
  66.8 0.0 collective-permute-done.21.refs_5_
  66.8 0.0 collective-permute-done.22.refs_6_
  66.9 7.9 %backward.1 = (bf16[64,4096]{1,0:T(8,128)(2,1)S(1)}, bf16[64,1024]{1,0:T(8,128)(2,1)S(1)}, bf16[64,1024]{1,0:T(8,128)(2,1)S(1)}, f32[32,4096]{1,0:T(8,128)S(1)}, bf16[32,4096]{1,0:T(8,128)(2,1)S(1)}) custom-call(bf16[8,4096]{1,0:T(8,128)(2,1)S(1)} %collective-permute-done.16.refs_0_, bf16[8,4096]{1,0:T(8,128)(2,1)S(1)} %collective-permute-done.17.refs_1_, ...), custom_call_target="tpu_custom_call" | custom-call | flops 1610612736 | bytes 25165824 | tf_op jit(solution)/shard_map/backward/pallas_call | solution.py:142
  74.8 0.5 collective-permute-start.24
  75.3 0.1 collective-permute-start.9
  75.4 12.5 %grads.1 = (bf16[4096,1024]{1,0:T(8,128)(2,1)}, bf16[4096,1024]{1,0:T(8,128)(2,1)}, bf16[1024,4096]{1,0:T(8,128)(2,1)}) custom-call(bf16[64,4096]{1,0:T(8,128)(2,1)S(1)} %get-tuple-element.34.tokens_ref, bf16[64,4096]{1,0:T(8,128)(2,1)S(1)} %get-tuple-element.35.cotangent_ref, bf16[64,1024]{1,0:T(8,128)(2,1)S(1)} %get-tuple-element.36.gate_delta_ref, ...), custom_call_target="tpu_custom_call" | custom-call | flops 1610612736 | bytes 25165824 | tf_op jit(solution)/shard_map/grads/pallas_call | solution.py:183
  87.9 0.7 collective-permute-start.25
  88.6 0.9 collective-permute-start.26
  89.5 3.9 %collective-permute-start.27 = (bf16[8,4096]{1,0:T(8,128)(2,1)S(1)}, bf16[8,4096]{1,0:T(8,128)(2,1)S(1)}, u32[]{:S(2)}, u32[]{:S(2)}) collective-permute-start(bf16[8,4096]{1,0:T(8,128)(2,1)S(1)} %get-tuple-element.47), channel_id=1, source_target_pairs={{0,10},{1,9},{2,8},{3,11},{4,14},{5,13},{6,12},{7,15},{8,2},{9,1},... | collective-permute-start | bytes 196616 | tf_op jit(solution)/shard_map/ppermute | solution.py:233
  93.4 0.9 collective-permute-start.28
  94.4 0.7 collective-permute-start.10
  95.1 0.7 collective-permute-start.11
  95.8 4.7 %collective-permute-start.12 = (bf16[8,4096]{1,0:T(8,128)(2,1)S(1)}, bf16[8,4096]{1,0:T(8,128)(2,1)S(1)}, u32[]{:S(2)}, u32[]{:S(2)}) collective-permute-start(bf16[8,4096]{1,0:T(8,128)(2,1)S(1)} %get-tuple-element.51), channel_id=1, source_target_pairs={{0,10},{1,9},{2,8},{3,11},{4,14},{5,13},{6,12},{7,15},{8,2},{9,1},... | collective-permute-start | bytes 196616 | tf_op jit(solution)/shard_map/ppermute | solution.py:233
  100.5 0.4 collective-permute-start.13
  101.0 1.1 collective-permute-start.29
  102.1 1.2 %collective-permute-done.12 = bf16[8,4096]{1,0:T(8,128)(2,1)S(1)} collective-permute-done((bf16[8,4096]{1,0:T(8,128)(2,1)S(1)}, bf16[8,4096]{1,0:T(8,128)(2,1)S(1)}, u32[]{:S(2)}, u32[]{:S(2)}) %collective-permute-start.12) | collective-permute-done | bytes 65568 | tf_op jit(solution)/shard_map/ppermute | solution.py:233
  103.3 4.3 %collective-permute-done.13 = bf16[8,4096]{1,0:T(8,128)(2,1)S(1)} collective-permute-done((bf16[8,4096]{1,0:T(8,128)(2,1)S(1)}, bf16[8,4096]{1,0:T(8,128)(2,1)S(1)}, u32[]{:S(2)}, u32[]{:S(2)}) %collective-permute-start.13) | collective-permute-done | bytes 65568 | tf_op jit(solution)/shard_map/ppermute | solution.py:233
  107.7 0.1 collective-permute-start.14
  107.7 0.6 fusion
  108.4 0.6 collective-permute-done.14
  109.0 0.6 fusion.1
  (40 shorter events, 0.4 us)
Async XLA Ops:
  16.1 7.9 %copy-start.4 = (bf16[4,4096]{1,0:T(4,128)(2,1)S(1)}, bf16[4,4096]{1,0:T(4,128)(2,1)}, u32[]{:S(2)}) copy-start(bf16[4,4096]{1,0:T(4,128)(2,1)} %param.6) | copy-start | bytes 98308
  16.1 8.4 %copy-start.5 = (bf16[4,4096]{1,0:T(4,128)(2,1)S(1)}, bf16[4,4096]{1,0:T(4,128)(2,1)}, u32[]{:S(2)}) copy-start(bf16[4,4096]{1,0:T(4,128)(2,1)} %param.7) | copy-start | bytes 98308
  16.1 27.8 %copy-start.6 = (s32[3,64,16]{1,2,0:T(8,128)S(1)}, s32[3,64,16]{1,2,0:T(8,128)}, u32[]{:S(2)}) copy-start(s32[3,64,16]{1,2,0:T(8,128)} %param.11) | copy-start | bytes 36868
  24.1 1.3 %collective-permute-start = (bf16[4,4096]{1,0:T(4,128)(2,1)S(1)}, bf16[4,4096]{1,0:T(4,128)(2,1)S(1)}, u32[]{:S(2)}, u32[]{:S(2)}) collective-permute-start(bf16[4,4096]{1,0:T(4,128)(2,1)S(1)} %copy-done.4), channel_id=1, source_target_pairs={{0,1},{1,0},{2,3},{3,2},{4,5},{5,4},{6,7},{7,6},{8,9},{9,8},{10,11... | collective-permute-start | bytes 98312 | tf_op jit(solution)/shard_map/ppermute | solution.py:224
  24.5 9.2 %collective-permute-start.15 = (bf16[4,4096]{1,0:T(4,128)(2,1)S(1)}, bf16[4,4096]{1,0:T(4,128)(2,1)S(1)}, u32[]{:S(2)}, u32[]{:S(2)}) collective-permute-start(bf16[4,4096]{1,0:T(4,128)(2,1)S(1)} %copy-done.5), channel_id=1, source_target_pairs={{0,1},{1,0},{2,3},{3,2},{4,5},{5,4},{6,7},{7,6},{8,9},{9,8},{10,11... | collective-permute-start | bytes 98312 | tf_op jit(solution)/shard_map/ppermute | solution.py:224
  25.4 9.2 %collective-permute-start.1 = (bf16[8,4096]{1,0:T(8,128)(2,1)S(1)}, bf16[8,4096]{1,0:T(8,128)(2,1)S(1)}, u32[]{:S(2)}, u32[]{:S(2)}) collective-permute-start(bf16[8,4096]{1,0:T(8,128)(2,1)S(1)} %pad_maximum_fusion), channel_id=1, source_target_pairs={{0,0},{1,3},{2,2},{3,1},{4,4},{5,7},{6,6},{7,5},{8,8},{9,11},{10,1... | collective-permute-start | bytes 196616 | tf_op jit(solution)/shard_map/ppermute | solution.py:225
  26.1 9.2 %collective-permute-start.2 = (bf16[8,4096]{1,0:T(8,128)(2,1)S(1)}, bf16[8,4096]{1,0:T(8,128)(2,1)S(1)}, u32[]{:S(2)}, u32[]{:S(2)}) collective-permute-start(bf16[8,4096]{1,0:T(8,128)(2,1)S(1)} %pad_maximum_fusion), channel_id=1, source_target_pairs={{0,6},{1,5},{2,4},{3,7},{4,2},{5,1},{6,0},{7,3},{8,14},{9,13},{10,... | collective-permute-start | bytes 196616 | tf_op jit(solution)/shard_map/ppermute | solution.py:225
  30.0 9.8 %collective-permute-start.3 = (bf16[8,4096]{1,0:T(8,128)(2,1)S(1)}, bf16[8,4096]{1,0:T(8,128)(2,1)S(1)}, u32[]{:S(2)}, u32[]{:S(2)}) collective-permute-start(bf16[8,4096]{1,0:T(8,128)(2,1)S(1)} %pad_maximum_fusion), channel_id=1, source_target_pairs={{0,10},{1,9},{2,8},{3,11},{4,14},{5,13},{6,12},{7,15},{8,2},{9,1},... | collective-permute-start | bytes 196616 | tf_op jit(solution)/shard_map/ppermute | solution.py:225
  32.5 7.2 %collective-permute-start.4 = (bf16[8,4096]{1,0:T(8,128)(2,1)S(1)}, bf16[8,4096]{1,0:T(8,128)(2,1)S(1)}, u32[]{:S(2)}, u32[]{:S(2)}) collective-permute-start(bf16[8,4096]{1,0:T(8,128)(2,1)S(1)} %pad_maximum_fusion), channel_id=1, source_target_pairs={{0,14},{1,13},{2,12},{3,15},{4,10},{5,9},{6,8},{7,11},{8,6},{9,5},... | collective-permute-start | bytes 196616 | tf_op jit(solution)/shard_map/ppermute | solution.py:225
  33.8 7.6 %collective-permute-start.16 = (bf16[8,4096]{1,0:T(8,128)(2,1)S(1)}, bf16[8,4096]{1,0:T(8,128)(2,1)S(1)}, u32[]{:S(2)}, u32[]{:S(2)}) collective-permute-start(bf16[8,4096]{1,0:T(8,128)(2,1)S(1)} %pad_maximum_fusion.1), channel_id=1, source_target_pairs={{0,0},{1,3},{2,2},{3,1},{4,4},{5,7},{6,6},{7,5},{8,8},{9,11},{10,1... | collective-permute-start | bytes 196616 | tf_op jit(solution)/shard_map/ppermute | solution.py:225
  34.6 6.8 %collective-permute-start.17 = (bf16[8,4096]{1,0:T(8,128)(2,1)S(1)}, bf16[8,4096]{1,0:T(8,128)(2,1)S(1)}, u32[]{:S(2)}, u32[]{:S(2)}) collective-permute-start(bf16[8,4096]{1,0:T(8,128)(2,1)S(1)} %pad_maximum_fusion.1), channel_id=1, source_target_pairs={{0,6},{1,5},{2,4},{3,7},{4,2},{5,1},{6,0},{7,3},{8,14},{9,13},{10,... | collective-permute-start | bytes 196616 | tf_op jit(solution)/shard_map/ppermute | solution.py:225
  35.3 8.7 %collective-permute-start.18 = (bf16[8,4096]{1,0:T(8,128)(2,1)S(1)}, bf16[8,4096]{1,0:T(8,128)(2,1)S(1)}, u32[]{:S(2)}, u32[]{:S(2)}) collective-permute-start(bf16[8,4096]{1,0:T(8,128)(2,1)S(1)} %pad_maximum_fusion.1), channel_id=1, source_target_pairs={{0,10},{1,9},{2,8},{3,11},{4,14},{5,13},{6,12},{7,15},{8,2},{9,1},... | collective-permute-start | bytes 196616 | tf_op jit(solution)/shard_map/ppermute | solution.py:225
  39.8 17.9 %collective-permute-start.19 = (bf16[8,4096]{1,0:T(8,128)(2,1)S(1)}, bf16[8,4096]{1,0:T(8,128)(2,1)S(1)}, u32[]{:S(2)}, u32[]{:S(2)}) collective-permute-start(bf16[8,4096]{1,0:T(8,128)(2,1)S(1)} %pad_maximum_fusion.1), channel_id=1, source_target_pairs={{0,14},{1,13},{2,12},{3,15},{4,10},{5,9},{6,8},{7,11},{8,6},{9,5},... | collective-permute-start | bytes 196616 | tf_op jit(solution)/shard_map/ppermute | solution.py:225
  39.8 18.5 %collective-permute-start.5 = (bf16[8,4096]{1,0:T(8,128)(2,1)S(1)}, bf16[8,4096]{1,0:T(8,128)(2,1)S(1)}, u32[]{:S(2)}, u32[]{:S(2)}) collective-permute-start(bf16[8,4096]{1,0:T(8,128)(2,1)S(1)} %collective-permute-done.1.refs_0_), channel_id=1, source_target_pairs={{0,1},{1,0},{2,3},{3,2},{4,5},{5,4},{6,7},{7,6},{8,9},{9,8},{10,11... | collective-permute-start | bytes 196616 | tf_op jit(solution)/shard_map/ppermute | solution.py:226
  41.4 17.0 %collective-permute-start.6 = (bf16[8,4096]{1,0:T(8,128)(2,1)S(1)}, bf16[8,4096]{1,0:T(8,128)(2,1)S(1)}, u32[]{:S(2)}, u32[]{:S(2)}) collective-permute-start(bf16[8,4096]{1,0:T(8,128)(2,1)S(1)} %collective-permute-done.2.refs_1_), channel_id=1, source_target_pairs={{0,1},{1,0},{2,3},{3,2},{4,5},{5,4},{6,7},{7,6},{8,9},{9,8},{10,11... | collective-permute-start | bytes 196616 | tf_op jit(solution)/shard_map/ppermute | solution.py:226
  41.4 17.4 %collective-permute-start.7 = (bf16[8,4096]{1,0:T(8,128)(2,1)S(1)}, bf16[8,4096]{1,0:T(8,128)(2,1)S(1)}, u32[]{:S(2)}, u32[]{:S(2)}) collective-permute-start(bf16[8,4096]{1,0:T(8,128)(2,1)S(1)} %collective-permute-done.3.refs_2_), channel_id=1, source_target_pairs={{0,1},{1,0},{2,3},{3,2},{4,5},{5,4},{6,7},{7,6},{8,9},{9,8},{10,11... | collective-permute-start | bytes 196616 | tf_op jit(solution)/shard_map/ppermute | solution.py:226
  44.0 14.9 %collective-permute-start.8 = (bf16[8,4096]{1,0:T(8,128)(2,1)S(1)}, bf16[8,4096]{1,0:T(8,128)(2,1)S(1)}, u32[]{:S(2)}, u32[]{:S(2)}) collective-permute-start(bf16[8,4096]{1,0:T(8,128)(2,1)S(1)} %collective-permute-done.4.refs_3_), channel_id=1, source_target_pairs={{0,1},{1,0},{2,3},{3,2},{4,5},{5,4},{6,7},{7,6},{8,9},{9,8},{10,11... | collective-permute-start | bytes 196616 | tf_op jit(solution)/shard_map/ppermute | solution.py:226
  44.2 5.8 %copy-start = (bf16[4096,1024]{1,0:T(8,128)(2,1)S(1)}, bf16[4096,1024]{1,0:T(8,128)(2,1)}, u32[]{:S(2)}) copy-start(bf16[4096,1024]{1,0:T(8,128)(2,1)} %copy.27.weight_ref) | copy-start | bytes 25165828
  44.2 3.5 %copy-start.1 = (bf16[4096,1024]{1,0:T(8,128)(2,1)S(1)}, bf16[4096,1024]{1,0:T(8,128)(2,1)}, u32[]{:S(2)}) copy-start(bf16[4096,1024]{1,0:T(8,128)(2,1)} %copy.26.weight_ref) | copy-start | bytes 25165828
  47.8 6.5 %slice-start = ((s8[8388608]{0:T(1024)(128)(4,1)}), s8[4194304]{0:T(1024)(128)(4,1)S(1)}, s32[]{:S(2)}) async-start(s8[8388608]{0:T(1024)(128)(4,1)} %bitcast.3), calls=%async_computation | async-start | bytes 8388608
  49.1 8.6 %copy-start.2 = (bf16[4096,1024]{1,0:T(8,128)(2,1)}, bf16[4096,1024]{1,0:T(8,128)(2,1)S(1)}, u32[]{:S(2)}) copy-start(bf16[4096,1024]{1,0:T(8,128)(2,1)S(1)} %get-tuple-element.25.refs_8_.refs_10_) | copy-start | bytes 25165828
  50.0 5.4 %slice-start.1 = ((s8[8388608]{0:T(1024)(128)(4,1)}), s8[4194304]{0:T(1024)(128)(4,1)S(1)}, s32[]{:S(2)}) async-start(s8[8388608]{0:T(1024)(128)(4,1)} %bitcast.3), calls=%async_computation.1 | async-start | bytes 8388608
  57.7 9.1 %collective-permute-start.20 = (bf16[8,4096]{1,0:T(8,128)(2,1)S(1)}, bf16[8,4096]{1,0:T(8,128)(2,1)S(1)}, u32[]{:S(2)}, u32[]{:S(2)}) collective-permute-start(bf16[8,4096]{1,0:T(8,128)(2,1)S(1)} %collective-permute-done.16.refs_0_), channel_id=1, source_target_pairs={{0,1},{1,0},{2,3},{3,2},{4,5},{5,4},{6,7},{7,6},{8,9},{9,8},{10,11... | collective-permute-start | bytes 196616 | tf_op jit(solution)/shard_map/ppermute | solution.py:226
  58.3 8.5 %collective-permute-start.21 = (bf16[8,4096]{1,0:T(8,128)(2,1)S(1)}, bf16[8,4096]{1,0:T(8,128)(2,1)S(1)}, u32[]{:S(2)}, u32[]{:S(2)}) collective-permute-start(bf16[8,4096]{1,0:T(8,128)(2,1)S(1)} %collective-permute-done.17.refs_1_), channel_id=1, source_target_pairs={{0,1},{1,0},{2,3},{3,2},{4,5},{5,4},{6,7},{7,6},{8,9},{9,8},{10,11... | collective-permute-start | bytes 196616 | tf_op jit(solution)/shard_map/ppermute | solution.py:226
  58.4 8.5 %collective-permute-start.22 = (bf16[8,4096]{1,0:T(8,128)(2,1)S(1)}, bf16[8,4096]{1,0:T(8,128)(2,1)S(1)}, u32[]{:S(2)}, u32[]{:S(2)}) collective-permute-start(bf16[8,4096]{1,0:T(8,128)(2,1)S(1)} %collective-permute-done.18.refs_2_), channel_id=1, source_target_pairs={{0,1},{1,0},{2,3},{3,2},{4,5},{5,4},{6,7},{7,6},{8,9},{9,8},{10,11... | collective-permute-start | bytes 196616 | tf_op jit(solution)/shard_map/ppermute | solution.py:226
  58.8 8.0 %collective-permute-start.23 = (bf16[8,4096]{1,0:T(8,128)(2,1)S(1)}, bf16[8,4096]{1,0:T(8,128)(2,1)S(1)}, u32[]{:S(2)}, u32[]{:S(2)}) collective-permute-start(bf16[8,4096]{1,0:T(8,128)(2,1)S(1)} %collective-permute-done.19.refs_3_), channel_id=1, source_target_pairs={{0,1},{1,0},{2,3},{3,2},{4,5},{5,4},{6,7},{7,6},{8,9},{9,8},{10,11... | collective-permute-start | bytes 196616 | tf_op jit(solution)/shard_map/ppermute | solution.py:226
  58.9 3.4 %copy-start.3 = (bf16[4096,1024]{1,0:T(8,128)(2,1)S(1)}, bf16[4096,1024]{1,0:T(8,128)(2,1)}, u32[]{:S(2)}) copy-start(bf16[4096,1024]{1,0:T(8,128)(2,1)} %copy-done.2) | copy-start | bytes 25165828
  74.8 13.0 %collective-permute-start.24 = (bf16[32,4096]{1,0:T(8,128)(2,1)S(1)}, bf16[32,4096]{1,0:T(8,128)(2,1)S(1)}, u32[]{:S(2)}, u32[]{:S(2)}) collective-permute-start(bf16[32,4096]{1,0:T(8,128)(2,1)S(1)} %get-tuple-element.33), channel_id=1, source_target_pairs={{0,1},{1,0},{2,3},{3,2},{4,5},{5,4},{6,7},{7,6},{8,9},{9,8},{10,11... | collective-permute-start | bytes 786440 | tf_op jit(solution)/shard_map/ppermute | solution.py:230
  75.3 19.0 %collective-permute-start.9 = (bf16[32,4096]{1,0:T(8,128)(2,1)S(1)}, bf16[32,4096]{1,0:T(8,128)(2,1)S(1)}, u32[]{:S(2)}, u32[]{:S(2)}) collective-permute-start(bf16[32,4096]{1,0:T(8,128)(2,1)S(1)} %get-tuple-element.29), channel_id=1, source_target_pairs={{0,1},{1,0},{2,3},{3,2},{4,5},{5,4},{6,7},{7,6},{8,9},{9,8},{10,11... | collective-permute-start | bytes 786440 | tf_op jit(solution)/shard_map/ppermute | solution.py:230
  87.9 7.1 %collective-permute-start.25 = (bf16[8,4096]{1,0:T(8,128)(2,1)S(1)}, bf16[8,4096]{1,0:T(8,128)(2,1)S(1)}, u32[]{:S(2)}, u32[]{:S(2)}) collective-permute-start(bf16[8,4096]{1,0:T(8,128)(2,1)S(1)} %get-tuple-element.45), channel_id=1, source_target_pairs={{0,0},{1,3},{2,2},{3,1},{4,4},{5,7},{6,6},{7,5},{8,8},{9,11},{10,1... | collective-permute-start | bytes 196616 | tf_op jit(solution)/shard_map/ppermute | solution.py:233
  88.6 7.2 %collective-permute-start.26 = (bf16[8,4096]{1,0:T(8,128)(2,1)S(1)}, bf16[8,4096]{1,0:T(8,128)(2,1)S(1)}, u32[]{:S(2)}, u32[]{:S(2)}) collective-permute-start(bf16[8,4096]{1,0:T(8,128)(2,1)S(1)} %get-tuple-element.48), channel_id=1, source_target_pairs={{0,6},{1,5},{2,4},{3,7},{4,2},{5,1},{6,0},{7,3},{8,14},{9,13},{10,... | collective-permute-start | bytes 196616 | tf_op jit(solution)/shard_map/ppermute | solution.py:233
  89.5 11.0 %collective-permute-start.27 = (bf16[8,4096]{1,0:T(8,128)(2,1)S(1)}, bf16[8,4096]{1,0:T(8,128)(2,1)S(1)}, u32[]{:S(2)}, u32[]{:S(2)}) collective-permute-start(bf16[8,4096]{1,0:T(8,128)(2,1)S(1)} %get-tuple-element.47), channel_id=1, source_target_pairs={{0,10},{1,9},{2,8},{3,11},{4,14},{5,13},{6,12},{7,15},{8,2},{9,1},... | collective-permute-start | bytes 196616 | tf_op jit(solution)/shard_map/ppermute | solution.py:233
  93.4 7.6 %collective-permute-start.28 = (bf16[8,4096]{1,0:T(8,128)(2,1)S(1)}, bf16[8,4096]{1,0:T(8,128)(2,1)S(1)}, u32[]{:S(2)}, u32[]{:S(2)}) collective-permute-start(bf16[8,4096]{1,0:T(8,128)(2,1)S(1)} %get-tuple-element.46), channel_id=1, source_target_pairs={{0,14},{1,13},{2,12},{3,15},{4,10},{5,9},{6,8},{7,11},{8,6},{9,5},... | collective-permute-start | bytes 196616 | tf_op jit(solution)/shard_map/ppermute | solution.py:233
  94.4 7.7 %collective-permute-start.10 = (bf16[8,4096]{1,0:T(8,128)(2,1)S(1)}, bf16[8,4096]{1,0:T(8,128)(2,1)S(1)}, u32[]{:S(2)}, u32[]{:S(2)}) collective-permute-start(bf16[8,4096]{1,0:T(8,128)(2,1)S(1)} %get-tuple-element.49), channel_id=1, source_target_pairs={{0,0},{1,3},{2,2},{3,1},{4,4},{5,7},{6,6},{7,5},{8,8},{9,11},{10,1... | collective-permute-start | bytes 196616 | tf_op jit(solution)/shard_map/ppermute | solution.py:233
  95.1 7.0 %collective-permute-start.11 = (bf16[8,4096]{1,0:T(8,128)(2,1)S(1)}, bf16[8,4096]{1,0:T(8,128)(2,1)S(1)}, u32[]{:S(2)}, u32[]{:S(2)}) collective-permute-start(bf16[8,4096]{1,0:T(8,128)(2,1)S(1)} %get-tuple-element.52), channel_id=1, source_target_pairs={{0,6},{1,5},{2,4},{3,7},{4,2},{5,1},{6,0},{7,3},{8,14},{9,13},{10,... | collective-permute-start | bytes 196616 | tf_op jit(solution)/shard_map/ppermute | solution.py:233
  95.8 7.5 %collective-permute-start.12 = (bf16[8,4096]{1,0:T(8,128)(2,1)S(1)}, bf16[8,4096]{1,0:T(8,128)(2,1)S(1)}, u32[]{:S(2)}, u32[]{:S(2)}) collective-permute-start(bf16[8,4096]{1,0:T(8,128)(2,1)S(1)} %get-tuple-element.51), channel_id=1, source_target_pairs={{0,10},{1,9},{2,8},{3,11},{4,14},{5,13},{6,12},{7,15},{8,2},{9,1},... | collective-permute-start | bytes 196616 | tf_op jit(solution)/shard_map/ppermute | solution.py:233
  100.5 7.1 %collective-permute-start.13 = (bf16[8,4096]{1,0:T(8,128)(2,1)S(1)}, bf16[8,4096]{1,0:T(8,128)(2,1)S(1)}, u32[]{:S(2)}, u32[]{:S(2)}) collective-permute-start(bf16[8,4096]{1,0:T(8,128)(2,1)S(1)} %get-tuple-element.50), channel_id=1, source_target_pairs={{0,14},{1,13},{2,12},{3,15},{4,10},{5,9},{6,8},{7,11},{8,6},{9,5},... | collective-permute-start | bytes 196616 | tf_op jit(solution)/shard_map/ppermute | solution.py:233
  101.0 6.7 %collective-permute-start.29 = (f32[4,4096]{1,0:T(4,128)S(1)}, f32[4,4096]{1,0:T(4,128)S(1)}, u32[]{:S(2)}, u32[]{:S(2)}) collective-permute-start(f32[4,4096]{1,0:T(4,128)S(1)} %slice.71), channel_id=1, source_target_pairs={{0,1},{1,0},{2,3},{3,2},{4,5},{5,4},{6,7},{7,6},{8,9},{9,8},{10,11... | collective-permute-start | bytes 196616 | tf_op jit(solution)/shard_map/ppermute | solution.py:236
  107.7 1.3 %collective-permute-start.14 = (f32[4,4096]{1,0:T(4,128)S(1)}, f32[4,4096]{1,0:T(4,128)S(1)}, u32[]{:S(2)}, u32[]{:S(2)}) collective-permute-start(f32[4,4096]{1,0:T(4,128)S(1)} %slice.65), channel_id=1, source_target_pairs={{0,1},{1,0},{2,3},{3,2},{4,5},{5,4},{6,7},{7,6},{8,9},{9,8},{10,11... | collective-permute-start | bytes 196616 | tf_op jit(solution)/shard_map/ppermute | solution.py:236

commit v2 on v1

v2 whole, which is shorter than its diff:
```python
import functools

import jax
import jax.numpy as jnp
from jax import lax
from jax.experimental import pallas as pl
from jax.experimental.pallas import tpu as pltpu
from jax.sharding import PartitionSpec as P

AXIS = "tensor"
BLOCK = 64
CHUNKS = 8
BF16 = jnp.bfloat16
F32 = jnp.float32
MIB = 2**20
VMEM = pl.BlockSpec(memory_space=pltpu.VMEM)


def dot(a, b, ca=1, cb=0):
    return lax.dot_general(a, b, (((ca,), (cb,)), ((), ())), preferred_element_type=F32)


def in_vmem(x):
    return pltpu.with_memory_space_constraint(x, pltpu.VMEM)


def in_hbm(x):
    return pltpu.with_memory_space_constraint(x, pltpu.HBM)


def shape(*dims, dtype=F32):
    return jax.ShapeDtypeStruct(dims, dtype)


def params(mib):
    return pltpu.CompilerParams(vmem_limit_bytes=mib * MIB)


def cost(flops, size):
    return pl.CostEstimate(flops=flops, bytes_accessed=size, transcendentals=0)


def spread(blocks, wide):
    row = lax.broadcasted_iota(jnp.int32, (blocks, wide), 0)
    column = lax.broadcasted_iota(jnp.int32, (blocks, wide), 1)
    return (row == column // BLOCK).astype(BF16)


def mask_kernel(flags_ref, *refs):
    weights, masked, keeps, sems = refs[:3], refs[3:6], refs[6:9], refs[9]
    copies = []
    for index, (weight_ref, masked_ref) in enumerate(zip(weights, masked)):
        rows = weight_ref.shape[0] // CHUNKS
        for chunk in range(CHUNKS):
            at = pl.ds(chunk * rows, rows)
            copies.append(
                pltpu.make_async_copy(weight_ref.at[at, :], masked_ref.at[at, :], sems.at[index, chunk])
            )
    for copy in copies:
        copy.start()
    for index, (masked_ref, keep_ref) in enumerate(zip(masked, keeps)):
        rows, columns = masked_ref.shape
        flags = flags_ref[index].astype(F32).astype(BF16)
        keep = dot(flags, spread(columns // BLOCK, columns), 0 if index == 2 else 1, 0)
        keep_ref[...] = keep
        keep = keep.astype(BF16)
        blocks = rows // BLOCK
        for block in range(blocks):
            if block * CHUNKS % blocks == 0:
                copies[index * CHUNKS + block * CHUNKS // blocks].wait()
            at = pl.ds(block * BLOCK, BLOCK)
            masked_ref[at, :] = masked_ref[at, :] * keep[block : block + 1, :]


def mask_weights(flags, *weights):
    hbm = pl.BlockSpec(memory_space=pltpu.HBM)
    return pl.pallas_call(
        mask_kernel,
        out_shape=tuple(pltpu.VMEM(w.shape, BF16) for w in weights)
        + tuple(shape(w.shape[0] // BLOCK, w.shape[1]) for w in weights),
        in_specs=[VMEM] + [hbm] * 3,
        out_specs=(VMEM,) * 6,
        scratch_shapes=[pltpu.SemaphoreType.DMA((3, CHUNKS))],
        compiler_params=params(8),
        cost_estimate=cost(0, sum(2 * w.size for w in weights)),
        name="mask",
    )(flags, *map(in_hbm, weights))


def layer_kernel(pieces, *refs):
    piece_refs = refs[:pieces]
    gate_ref, up_ref, down_ref = refs[pieces : pieces + 3]
    tokens_ref, cotangents_ref, gate_delta_ref, up_delta_ref, hidden_t_ref, mine_ref, theirs_ref = refs[
        pieces + 3 : pieces + 10
    ]
    hidden_ref = refs[pieces + 10]
    features, units = gate_ref.shape
    both = [piece[...] for piece in piece_refs]
    tokens_ref[...] = jnp.concatenate([piece[: piece.shape[0] // 2] for piece in both], 0)
    cotangents_ref[...] = jnp.concatenate([piece[piece.shape[0] // 2 :] for piece in both], 0)
    for start in range(0, units, 256):
        at = pl.ds(start, 256)
        gate = dot(tokens_ref[...], gate_ref[:, at])
        up = dot(tokens_ref[...], up_ref[:, at])
        hidden_grad = dot(cotangents_ref[...], down_ref[at, :], 1, 1)
        sig = jax.nn.sigmoid(gate)
        act = gate * sig
        hidden = act * up
        hidden_ref[:, at] = hidden.astype(BF16)
        hidden_t_ref[at, :] = hidden.T.astype(BF16)
        gate_delta_ref[:, at] = (hidden_grad * up * sig * (1.0 + gate * (1.0 - sig))).astype(BF16)
        up_delta_ref[:, at] = (hidden_grad * act).astype(BF16)
    half = tokens_ref.shape[0] // 2
    for start in range(0, features, 512):
        at = pl.ds(start, 512)
        mixed = dot(hidden_ref[...], down_ref[:, at])
        mine_ref[:, at] = mixed[:half]
        theirs_ref[:, at] = mixed[half:].astype(BF16)
        grad = dot(gate_delta_ref[...], gate_ref[at, :], 1, 1)
        grad += dot(up_delta_ref[...], up_ref[at, :], 1, 1)
        at = pl.ds(features + start, 512)
        mine_ref[:, at] = grad[:half]
        theirs_ref[:, at] = grad[half:].astype(BF16)


def layer(pieces, gate, up, down):
    rows = sum(piece.shape[0] for piece in pieces) // 2
    features, units = gate.shape
    return pl.pallas_call(
        functools.partial(layer_kernel, len(pieces)),
        out_shape=(
            shape(rows, features, dtype=BF16),
            shape(rows, features, dtype=BF16),
            shape(rows, units, dtype=BF16),
            shape(rows, units, dtype=BF16),
            shape(units, rows, dtype=BF16),
            shape(rows // 2, 2 * features),
            shape(rows // 2, 2 * features, dtype=BF16),
        ),
        in_specs=[VMEM] * (len(pieces) + 3),
        out_specs=(VMEM,) * 7,
        scratch_shapes=[pltpu.VMEM((rows, units), BF16)],
        compiler_params=params(16),
        cost_estimate=cost(12 * rows * features * units, 3 * 2 * features * units),
        name="layer",
    )(*pieces, *map(in_vmem, (gate, up, down)))


def grads_kernel(
    tokens_ref, cotangent_ref, gate_delta_ref, up_delta_ref, hidden_t_ref, keep_g_ref, keep_u_ref, keep_d_ref,
    gate_ref, up_ref, down_ref,
):
    step = pl.program_id(0)
    blocks = gate_ref.shape[0] // BLOCK
    for delta_ref, keep_ref, out_ref in (
        (gate_delta_ref, keep_g_ref, gate_ref),
        (up_delta_ref, keep_u_ref, up_ref),
    ):
        grad = dot(tokens_ref[...], delta_ref[...], 0, 0)
        for block in range(blocks):
            keep = keep_ref[pl.ds(step * blocks + block, 1), :]
            at = slice(block * BLOCK, (block + 1) * BLOCK)
            out_ref[at, :] = (grad[at, :] * keep).astype(BF16)
    grad = dot(hidden_t_ref[...], cotangent_ref[...])
    down_ref[...] = (grad * keep_d_ref[pl.ds(step, 1), :]).astype(BF16)


def grads(tokens, cotangents, gate_delta, up_delta, hidden_t, keeps):
    rows, features = tokens.shape
    units = hidden_t.shape[0]
    steps = units // BLOCK
    wide = features // steps
    return pl.pallas_call(
        grads_kernel,
        grid=(steps,),
        out_shape=(
            shape(features, units, dtype=BF16),
            shape(features, units, dtype=BF16),
            shape(units, features, dtype=BF16),
        ),
        in_specs=[
            pl.BlockSpec((rows, wide), lambda i: (0, i)),
            VMEM,
            VMEM,
            VMEM,
            pl.BlockSpec((BLOCK, rows), lambda i: (i, 0)),
            VMEM,
            VMEM,
            VMEM,
        ],
        out_specs=(
            pl.BlockSpec((wide, units), lambda i: (i, 0)),
            pl.BlockSpec((wide, units), lambda i: (i, 0)),
            pl.BlockSpec((BLOCK, features), lambda i: (i, 0)),
        ),
        compiler_params=params(16),
        cost_estimate=cost(6 * rows * features * units, 3 * 2 * features * units),
        name="grads",
    )(tokens, cotangents, gate_delta, up_delta, hidden_t, *keeps)


def across_cores(devices):
    return [(i, i ^ 1) for i in range(devices)]


def across_chips(devices):
    def pairs(offsets):
        return [(i, ((i // 2) ^ offsets[i % 2]) * 2 + i % 2) for i in range(devices)]

    return [pairs((k + 1, k) if k else (0, 1)) for k in range(0, devices // 2, 2)]


def gather(own, devices, after):
    mine = [lax.ppermute(own, AXIS, pairs) for pairs in across_chips(devices)]
    *mine, after = lax.optimization_barrier((*mine, after))
    return mine + [lax.ppermute(piece, AXIS, across_cores(devices)) for piece in mine], after


def scatter(total, devices, after):
    chips = across_chips(devices)
    rows = total.shape[0] // len(chips)
    parts = [lax.ppermute(total[k * rows : (k + 1) * rows], AXIS, pairs) for k, pairs in enumerate(chips)]
    *parts, after = lax.optimization_barrier((*parts, after))
    part = sum(p.astype(F32) for p in parts)
    half = rows // 2
    return (part[:half] + lax.ppermute(part[half:], AXIS, across_cores(devices))).astype(BF16), after


def shards(devices, tokens, cotangent, gate_weight, up_weight, down_weight, block_mask):
    features = tokens.shape[1]
    cores = across_cores(devices)
    own = jnp.concatenate(
        [tokens, lax.ppermute(tokens, AXIS, cores), cotangent, lax.ppermute(cotangent, AXIS, cores)], 0
    )
    own, block_mask = lax.optimization_barrier((own, block_mask))
    gate, up, down, *keeps = mask_weights(block_mask, gate_weight, up_weight, down_weight)
    pieces, keeps[0] = gather(own, devices, keeps[0])
    all_tokens, all_cotangents, gate_delta, up_delta, hidden_t, mine, theirs = layer(pieces, gate, up, down)
    total = (mine + lax.ppermute(theirs, AXIS, cores).astype(F32)).astype(BF16)
    total, hidden_t = lax.optimization_barrier((total, hidden_t))
    gate_grad, up_grad, down_grad = grads(all_tokens, all_cotangents, gate_delta, up_delta, hidden_t, keeps)
    sums, down_grad = scatter(total, devices, down_grad)
    return sums[:, :features], sums[:, features:], gate_grad, up_grad, down_grad


def solution(mesh):
    in_specs = (
        P(("group", AXIS), None),
        P(("group", AXIS), None),
        P(None, AXIS),
        P(None, AXIS),
        P(AXIS, None),
        P(None, None, AXIS),
    )
    out_specs = (
        P(("group", AXIS), None),
        P(("group", AXIS), None),
        P(None, ("group", AXIS)),
        P(None, ("group", AXIS)),
        P(("group", AXIS), None),
    )
    body = functools.partial(shards, mesh.shape[AXIS])
    return jax.shard_map(body, mesh=mesh, in_specs=in_specs, out_specs=out_specs, check_vma=False)
```

time: 110 us -> 57.9 us (0.53)
  local copies, waits for them, and re-layouts: 35.7 us -> 1.54 us
  starting transfers between devices: 32.7 us -> 16.3 us
  waiting for transfers between devices: 9.04 us -> 5.33 us
  Pallas kernels: 29.7 us -> 32.7 us
    unnamed x24 -> x0, local copies, waits for them, and re-layouts: 35.6 us -> none
    ppermute x8 -> x4, starting transfers between devices: 12.9 us -> 5.95 us  [scatter(): lax.ppermute(total[k * rows:(k + 1) * rows], AXIS, pairs)]
    ppermute x8 -> x4, starting transfers between devices: 14.3 us -> 8.12 us  [gather(): mine = [lax.ppermute(own, AXIS, pairs) for pairs in across_chips(devices)]]
    ppermute x8 -> x4, waiting for transfers between devices: 5.5 us -> 0.01 us  [scatter(): lax.ppermute(total[k * rows:(k + 1) * rows], AXIS, pairs)]
    pallas_call x5 -> x2, Pallas kernels: 17.3 us -> 20.2 us  [the longest x1 11.7 us: layer(): pl.pallas_call(functools.partial(layer_kernel, len(pieces)), out_shape=(s...]
    ppermute x4 -> x3, waiting for transfers between devices: 0.79 us -> 3.01 us  [the longest x1 1.67 us: shards(): total = (mine + lax.ppermute(theirs, AXIS, cores).astype(F32)).astype(BF16)]
    ppermute x8 -> x4, starting transfers between devices: 3.25 us -> 1.09 us  [gather(): lax.ppermute(piece, AXIS, across_cores(devices))]
    ppermute x8 -> x4, waiting for transfers between devices: 2.13 us -> 0.01 us  [gather(): mine = [lax.ppermute(own, AXIS, pairs) for pairs in across_chips(devices)]]
  transfers between devices with their start and end apart: 30 -> 16, of which waited for: 5 -> 8; matrix products, arithmetic and copies ran while one was open for 1% -> 1% of each run, Pallas kernels for 20% -> 36%
where the time goes in v2:
time: 57.9 us; the launch traced here: 57.6 us
  Pallas kernels  32.7 us (56%)
  starting transfers between devices  16.3 us (28%)
  waiting for transfers between devices  5.33 us (9%)
  local copies, waits for them, and re-layouts  1.54 us (3%)
  other arithmetic  1.04 us (2%)
  between operations  0.75 us (1%)
    pallas_call x1, Pallas kernels, grads(): pl.pallas_call(grads_kernel, grid=(steps,), out_shape=(shape(features, un...  12.5 us
    pallas_call x1, Pallas kernels, layer(): pl.pallas_call(functools.partial(layer_kernel, len(pieces)), out_shape=(s...  11.7 us
    pallas_call x1, Pallas kernels, mask_weights(): pl.pallas_call(mask_kernel, out_shape=tuple((pltpu.VMEM(w.shape, BF16) fo...  8.48 us
    ppermute x4, starting transfers between devices, gather(): mine = [lax.ppermute(own, AXIS, pairs) for pairs in across_chips(devices)]  8.12 us
    ppermute x4, starting transfers between devices, scatter(): lax.ppermute(total[k * rows:(k + 1) * rows], AXIS, pairs)  5.95 us
    ppermute x1, waiting for transfers between devices, shards(): total = (mine + lax.ppermute(theirs, AXIS, cores).astype(F32)).astype(BF16)  1.67 us
    ppermute x1, waiting for transfers between devices, scatter(): lax.ppermute(part[half:], AXIS, across_cores(devices))  1.2 us
  transfers between devices with their start and end apart: 16, of which 8 were waited for; matrix products, arithmetic and copies ran while one was open for 1% of the time, Pallas kernels for 36%

profile of v2, /device:TPU:0, one launch (start us, length us, event | category | flops | bytes accessed | tf_op | source)
XLA Modules:
  0.0 57.6 jit_solution(2950225709377527616)
XLA Ops:
  0.6 0.5 collective-permute-start
  1.1 0.1 collective-permute-start.1
  1.2 1.0 %collective-permute-done = bf16[4,4096]{1,0:T(4,128)(2,1)S(1)} collective-permute-done((bf16[4,4096]{1,0:T(4,128)(2,1)}, bf16[4,4096]{1,0:T(4,128)(2,1)S(1)}, u32[]{:S(2)}, u32[]{:S(2)}) %collective-permute-start) | collective-permute-done | bytes 32800 | tf_op jit(solution)/shard_map/ppermute | solution.py:233
  2.2 0.3 collective-permute-done.1
  2.6 0.9 %pad_maximum_fusion = bf16[16,4096]{1,0:T(8,128)(2,1)S(1)} fusion(bf16[4,4096]{1,0:T(4,128)(2,1)S(1)} %collective-permute-done.1, bf16[4,4096]{1,0:T(4,128)(2,1)} %param.7, bf16[4,4096]{1,0:T(4,128)(2,1)S(1)} %collective-permute-done, bf16[4,4096]{1,0:T(4,128)(2,1)} %param.6), kind=kLoop, calls=%fused_computation.4 | loop fusion | flops 524288 | bytes 262144 | tf_op jit(solution)/shard_map/concatenate | solution.py:232
  3.4 5.8 %collective-permute-start.5 = (bf16[16,4096]{1,0:T(8,128)(2,1)S(1)}, bf16[16,4096]{1,0:T(8,128)(2,1)S(1)}, u32[]{:S(2)}, u32[]{:S(2)}) collective-permute-start(bf16[16,4096]{1,0:T(8,128)(2,1)S(1)} %pad_maximum_fusion), channel_id=1, source_target_pairs={{0,14},{1,13},{2,12},{3,15},{4,10},{5,9},{6,8},{7,11},{8,6},{9,5},... | collective-permute-start | bytes 393224 | tf_op jit(solution)/shard_map/ppermute | solution.py:214
  9.2 0.0 collective-permute-start.4
  9.2 1.7 %collective-permute-start.3 = (bf16[16,4096]{1,0:T(8,128)(2,1)S(1)}, bf16[16,4096]{1,0:T(8,128)(2,1)S(1)}, u32[]{:S(2)}, u32[]{:S(2)}) collective-permute-start(bf16[16,4096]{1,0:T(8,128)(2,1)S(1)} %pad_maximum_fusion), channel_id=1, source_target_pairs={{0,6},{1,5},{2,4},{3,7},{4,2},{5,1},{6,0},{7,3},{8,14},{9,13},{10,... | collective-permute-start | bytes 393224 | tf_op jit(solution)/shard_map/ppermute | solution.py:214
  10.9 0.7 %collective-permute-start.2 = (bf16[16,4096]{1,0:T(8,128)(2,1)S(1)}, bf16[16,4096]{1,0:T(8,128)(2,1)S(1)}, u32[]{:S(2)}, u32[]{:S(2)}) collective-permute-start(bf16[16,4096]{1,0:T(8,128)(2,1)S(1)} %pad_maximum_fusion), channel_id=1, source_target_pairs={{0,0},{1,3},{2,2},{3,1},{4,4},{5,7},{6,6},{7,5},{8,8},{9,11},{10,1... | collective-permute-start | bytes 393224 | tf_op jit(solution)/shard_map/ppermute | solution.py:214
  11.6 0.8 %copy.11.flags_ref = s32[3,64,16]{2,1,0:T(8,128)S(1)} copy(s32[3,64,16]{1,2,0:T(8,128)} %param.11) | data formatting | bytes 24576 | tf_op jit(solution)/shard_map/optimization_barrier | solution.py:235
  12.4 8.5 %mask.1 = (bf16[4096,1024]{1,0:T(8,128)(2,1)S(1)}, bf16[4096,1024]{1,0:T(8,128)(2,1)S(1)}, bf16[1024,4096]{1,0:T(8,128)(2,1)S(1)}, f32[64,1024]{1,0:T(8,128)S(1)...) custom-call(s32[3,64,16]{2,1,0:T(8,128)S(1)} %copy.11.flags_ref, bf16[4096,1024]{1,0:T(8,128)(2,1)} %refs_0_.1, ...), custom_call_target="tpu_custom_call" | custom-call | bytes 25165824 | tf_op jit(solution)/shard_map/mask/pallas_call | solution.py:77
  20.9 0.0 collective-permute-done.5.refs_3_
  20.9 0.0 collective-permute-done.4.refs_2_
  20.9 0.0 collective-permute-done.3.refs_1_
  20.9 0.0 collective-permute-done.2.refs_0_
  20.9 0.3 collective-permute-start.6
  21.3 0.2 collective-permute-start.7
  21.5 0.3 collective-permute-start.8
  21.8 0.2 collective-permute-start.9
  22.0 0.3 collective-permute-done.6.refs_4_
  22.3 0.3 collective-permute-done.7.refs_5_
  22.6 0.2 collective-permute-done.8.refs_6_
  22.8 0.3 collective-permute-done.9.refs_7_
  23.1 11.7 %layer.1 = (bf16[64,4096]{1,0:T(8,128)(2,1)S(1)}, bf16[64,4096]{1,0:T(8,128)(2,1)S(1)}, bf16[64,1024]{1,0:T(8,128)(2,1)S(1)}, bf16[64,1024]{1,0:T(8,128)(2,1)S(1...) custom-call(bf16[16,4096]{1,0:T(8,128)(2,1)S(1)} %collective-permute-done.2.refs_0_, ...), custom_call_target="tpu_custom_call" | custom-call | flops 3221225472 | bytes 25165824 | tf_op jit(solution)/shard_map/layer/pallas_call | solution.py:129
  34.8 0.3 collective-permute-start.10
  35.1 1.7 %collective-permute-done.10 = bf16[32,8192]{1,0:T(8,128)(2,1)S(1)} collective-permute-done((bf16[32,8192]{1,0:T(8,128)(2,1)S(1)}, bf16[32,8192]{1,0:T(8,128)(2,1)S(1)}, u32[]{:S(2)}, u32[]{:S(2)}) %collective-permute-start.10) | collective-permute-done | bytes 524320 | tf_op jit(solution)/shard_map/ppermute | solution.py:239
  36.8 0.1 add_convert_fusion
  36.9 3.5 %collective-permute-start.14 = (bf16[8,8192]{1,0:T(8,128)(2,1)S(1)}, bf16[8,8192]{1,0:T(8,128)(2,1)S(1)}, u32[]{:S(2)}, u32[]{:S(2)}) collective-permute-start(bf16[8,8192]{1,0:T(8,128)(2,1)S(1)} %get-tuple-element.65), channel_id=1, source_target_pairs={{0,14},{1,13},{2,12},{3,15},{4,10},{5,9},{6,8},{7,11},{8,6},{9,5},... | collective-permute-start | bytes 393224 | tf_op jit(solution)/shard_map/ppermute | solution.py:222
  40.5 0.3 collective-permute-start.13
  40.7 1.5 %collective-permute-start.12 = (bf16[8,8192]{1,0:T(8,128)(2,1)S(1)}, bf16[8,8192]{1,0:T(8,128)(2,1)S(1)}, u32[]{:S(2)}, u32[]{:S(2)}) collective-permute-start(bf16[8,8192]{1,0:T(8,128)(2,1)S(1)} %get-tuple-element.67), channel_id=1, source_target_pairs={{0,6},{1,5},{2,4},{3,7},{4,2},{5,1},{6,0},{7,3},{8,14},{9,13},{10,... | collective-permute-start | bytes 393224 | tf_op jit(solution)/shard_map/ppermute | solution.py:222
  42.2 0.7 %collective-permute-start.11 = (bf16[8,8192]{1,0:T(8,128)(2,1)S(1)}, bf16[8,8192]{1,0:T(8,128)(2,1)S(1)}, u32[]{:S(2)}, u32[]{:S(2)}) collective-permute-start(bf16[8,8192]{1,0:T(8,128)(2,1)S(1)} %get-tuple-element.68), channel_id=1, source_target_pairs={{0,0},{1,3},{2,2},{3,1},{4,4},{5,7},{6,6},{7,5},{8,8},{9,11},{10,1... | collective-permute-start | bytes 393224 | tf_op jit(solution)/shard_map/ppermute | solution.py:222
  42.9 12.5 %grads.1 = (bf16[4096,1024]{1,0:T(8,128)(2,1)}, bf16[4096,1024]{1,0:T(8,128)(2,1)}, bf16[1024,4096]{1,0:T(8,128)(2,1)}) custom-call(bf16[64,4096]{1,0:T(8,128)(2,1)S(1)} %get-tuple-element.49.tokens_ref, bf16[64,4096]{1,0:T(8,128)(2,1)S(1)} %get-tuple-element.50.cotangent_ref, bf16[64,1024]{1,0:T(8,128)(2,1)S(1)} %get-tuple-element.51.gate_delta_ref, ...), custom_call_target="tpu_custom_call" | custom-call | flops 1610612736 | bytes 25165824 | tf_op jit(solution)/shard_map/grads/pallas_call | solution.py:173
  55.4 0.0 collective-permute-done.14
  55.4 0.0 collective-permute-done.13
  55.4 0.0 collective-permute-done.12
  55.4 0.0 collective-permute-done.11
  55.4 0.1 convert_add_fusion
  55.5 0.2 collective-permute-start.15
  55.8 1.2 %collective-permute-done.15 = f32[4,8192]{1,0:T(4,128)S(1)} collective-permute-done((f32[4,8192]{1,0:T(4,128)S(1)}, f32[4,8192]{1,0:T(4,128)S(1)}, u32[]{:S(2)}, u32[]{:S(2)}) %collective-permute-start.15) | collective-permute-done | bytes 131104 | tf_op jit(solution)/shard_map/ppermute | solution.py:226
  57.0 0.7 %fusion.2 = (bf16[4,4096]{1,0:T(4,128)(2,1)}, bf16[4,4096]{1,0:T(4,128)(2,1)}) fusion(bf16[4,8192]{1,0:T(4,128)(2,1)S(1)} %fusion), kind=kLoop, calls=%fused_computation.6 | loop fusion | bytes 131072 | tf_op jit(solution)/shard_map/slice | solution.py:243
  (3 shorter events, 0.1 us)
Async XLA Ops:
  0.6 1.6 %collective-permute-start = (bf16[4,4096]{1,0:T(4,128)(2,1)}, bf16[4,4096]{1,0:T(4,128)(2,1)S(1)}, u32[]{:S(2)}, u32[]{:S(2)}) collective-permute-start(bf16[4,4096]{1,0:T(4,128)(2,1)} %param.6), channel_id=1, source_target_pairs={{0,1},{1,0},{2,3},{3,2},{4,5},{5,4},{6,7},{7,6},{8,9},{9,8},{10,11... | collective-permute-start | bytes 98312 | tf_op jit(solution)/shard_map/ppermute | solution.py:233
  1.1 1.4 %collective-permute-start.1 = (bf16[4,4096]{1,0:T(4,128)(2,1)}, bf16[4,4096]{1,0:T(4,128)(2,1)S(1)}, u32[]{:S(2)}, u32[]{:S(2)}) collective-permute-start(bf16[4,4096]{1,0:T(4,128)(2,1)} %param.7), channel_id=1, source_target_pairs={{0,1},{1,0},{2,3},{3,2},{4,5},{5,4},{6,7},{7,6},{8,9},{9,8},{10,11... | collective-permute-start | bytes 98312 | tf_op jit(solution)/shard_map/ppermute | solution.py:233
  3.4 17.5 %collective-permute-start.5 = (bf16[16,4096]{1,0:T(8,128)(2,1)S(1)}, bf16[16,4096]{1,0:T(8,128)(2,1)S(1)}, u32[]{:S(2)}, u32[]{:S(2)}) collective-permute-start(bf16[16,4096]{1,0:T(8,128)(2,1)S(1)} %pad_maximum_fusion), channel_id=1, source_target_pairs={{0,14},{1,13},{2,12},{3,15},{4,10},{5,9},{6,8},{7,11},{8,6},{9,5},... | collective-permute-start | bytes 393224 | tf_op jit(solution)/shard_map/ppermute | solution.py:214
  9.2 11.7 %collective-permute-start.4 = (bf16[16,4096]{1,0:T(8,128)(2,1)S(1)}, bf16[16,4096]{1,0:T(8,128)(2,1)S(1)}, u32[]{:S(2)}, u32[]{:S(2)}) collective-permute-start(bf16[16,4096]{1,0:T(8,128)(2,1)S(1)} %pad_maximum_fusion), channel_id=1, source_target_pairs={{0,10},{1,9},{2,8},{3,11},{4,14},{5,13},{6,12},{7,15},{8,2},{9,1},... | collective-permute-start | bytes 393224 | tf_op jit(solution)/shard_map/ppermute | solution.py:214
  9.2 11.7 %collective-permute-start.3 = (bf16[16,4096]{1,0:T(8,128)(2,1)S(1)}, bf16[16,4096]{1,0:T(8,128)(2,1)S(1)}, u32[]{:S(2)}, u32[]{:S(2)}) collective-permute-start(bf16[16,4096]{1,0:T(8,128)(2,1)S(1)} %pad_maximum_fusion), channel_id=1, source_target_pairs={{0,6},{1,5},{2,4},{3,7},{4,2},{5,1},{6,0},{7,3},{8,14},{9,13},{10,... | collective-permute-start | bytes 393224 | tf_op jit(solution)/shard_map/ppermute | solution.py:214
  10.9 10.0 %collective-permute-start.2 = (bf16[16,4096]{1,0:T(8,128)(2,1)S(1)}, bf16[16,4096]{1,0:T(8,128)(2,1)S(1)}, u32[]{:S(2)}, u32[]{:S(2)}) collective-permute-start(bf16[16,4096]{1,0:T(8,128)(2,1)S(1)} %pad_maximum_fusion), channel_id=1, source_target_pairs={{0,0},{1,3},{2,2},{3,1},{4,4},{5,7},{6,6},{7,5},{8,8},{9,11},{10,1... | collective-permute-start | bytes 393224 | tf_op jit(solution)/shard_map/ppermute | solution.py:214
  20.9 1.4 %collective-permute-start.6 = (bf16[16,4096]{1,0:T(8,128)(2,1)S(1)}, bf16[16,4096]{1,0:T(8,128)(2,1)S(1)}, u32[]{:S(2)}, u32[]{:S(2)}) collective-permute-start(bf16[16,4096]{1,0:T(8,128)(2,1)S(1)} %collective-permute-done.2.refs_0_), channel_id=1, source_target_pairs={{0,1},{1,0},{2,3},{3,2},{4,5},{5,4},{6,7},{7,6},{8,9},{9,8},{10,11... | collective-permute-start | bytes 393224 | tf_op jit(solution)/shard_map/ppermute | solution.py:216
  21.3 1.3 %collective-permute-start.7 = (bf16[16,4096]{1,0:T(8,128)(2,1)S(1)}, bf16[16,4096]{1,0:T(8,128)(2,1)S(1)}, u32[]{:S(2)}, u32[]{:S(2)}) collective-permute-start(bf16[16,4096]{1,0:T(8,128)(2,1)S(1)} %collective-permute-done.3.refs_1_), channel_id=1, source_target_pairs={{0,1},{1,0},{2,3},{3,2},{4,5},{5,4},{6,7},{7,6},{8,9},{9,8},{10,11... | collective-permute-start | bytes 393224 | tf_op jit(solution)/shard_map/ppermute | solution.py:216
  21.5 1.3 %collective-permute-start.8 = (bf16[16,4096]{1,0:T(8,128)(2,1)S(1)}, bf16[16,4096]{1,0:T(8,128)(2,1)S(1)}, u32[]{:S(2)}, u32[]{:S(2)}) collective-permute-start(bf16[16,4096]{1,0:T(8,128)(2,1)S(1)} %collective-permute-done.4.refs_2_), channel_id=1, source_target_pairs={{0,1},{1,0},{2,3},{3,2},{4,5},{5,4},{6,7},{7,6},{8,9},{9,8},{10,11... | collective-permute-start | bytes 393224 | tf_op jit(solution)/shard_map/ppermute | solution.py:216
  21.8 1.3 %collective-permute-start.9 = (bf16[16,4096]{1,0:T(8,128)(2,1)S(1)}, bf16[16,4096]{1,0:T(8,128)(2,1)S(1)}, u32[]{:S(2)}, u32[]{:S(2)}) collective-permute-start(bf16[16,4096]{1,0:T(8,128)(2,1)S(1)} %collective-permute-done.5.refs_3_), channel_id=1, source_target_pairs={{0,1},{1,0},{2,3},{3,2},{4,5},{5,4},{6,7},{7,6},{8,9},{9,8},{10,11... | collective-permute-start | bytes 393224 | tf_op jit(solution)/shard_map/ppermute | solution.py:216
  34.8 2.0 %collective-permute-start.10 = (bf16[32,8192]{1,0:T(8,128)(2,1)S(1)}, bf16[32,8192]{1,0:T(8,128)(2,1)S(1)}, u32[]{:S(2)}, u32[]{:S(2)}) collective-permute-start(bf16[32,8192]{1,0:T(8,128)(2,1)S(1)} %get-tuple-element.46), channel_id=1, source_target_pairs={{0,1},{1,0},{2,3},{3,2},{4,5},{5,4},{6,7},{7,6},{8,9},{9,8},{10,11... | collective-permute-start | bytes 1572872 | tf_op jit(solution)/shard_map/ppermute | solution.py:239
  36.9 18.5 %collective-permute-start.14 = (bf16[8,8192]{1,0:T(8,128)(2,1)S(1)}, bf16[8,8192]{1,0:T(8,128)(2,1)S(1)}, u32[]{:S(2)}, u32[]{:S(2)}) collective-permute-start(bf16[8,8192]{1,0:T(8,128)(2,1)S(1)} %get-tuple-element.65), channel_id=1, source_target_pairs={{0,14},{1,13},{2,12},{3,15},{4,10},{5,9},{6,8},{7,11},{8,6},{9,5},... | collective-permute-start | bytes 393224 | tf_op jit(solution)/shard_map/ppermute | solution.py:222
  40.5 15.0 %collective-permute-start.13 = (bf16[8,8192]{1,0:T(8,128)(2,1)S(1)}, bf16[8,8192]{1,0:T(8,128)(2,1)S(1)}, u32[]{:S(2)}, u32[]{:S(2)}) collective-permute-start(bf16[8,8192]{1,0:T(8,128)(2,1)S(1)} %get-tuple-element.66), channel_id=1, source_target_pairs={{0,10},{1,9},{2,8},{3,11},{4,14},{5,13},{6,12},{7,15},{8,2},{9,1},... | collective-permute-start | bytes 393224 | tf_op jit(solution)/shard_map/ppermute | solution.py:222
  40.7 14.7 %collective-permute-start.12 = (bf16[8,8192]{1,0:T(8,128)(2,1)S(1)}, bf16[8,8192]{1,0:T(8,128)(2,1)S(1)}, u32[]{:S(2)}, u32[]{:S(2)}) collective-permute-start(bf16[8,8192]{1,0:T(8,128)(2,1)S(1)} %get-tuple-element.67), channel_id=1, source_target_pairs={{0,6},{1,5},{2,4},{3,7},{4,2},{5,1},{6,0},{7,3},{8,14},{9,13},{10,... | collective-permute-start | bytes 393224 | tf_op jit(solution)/shard_map/ppermute | solution.py:222
  42.2 13.2 %collective-permute-start.11 = (bf16[8,8192]{1,0:T(8,128)(2,1)S(1)}, bf16[8,8192]{1,0:T(8,128)(2,1)S(1)}, u32[]{:S(2)}, u32[]{:S(2)}) collective-permute-start(bf16[8,8192]{1,0:T(8,128)(2,1)S(1)} %get-tuple-element.68), channel_id=1, source_target_pairs={{0,0},{1,3},{2,2},{3,1},{4,4},{5,7},{6,6},{7,5},{8,8},{9,11},{10,1... | collective-permute-start | bytes 393224 | tf_op jit(solution)/shard_map/ppermute | solution.py:222
  55.5 1.4 %collective-permute-start.15 = (f32[4,8192]{1,0:T(4,128)S(1)}, f32[4,8192]{1,0:T(4,128)S(1)}, u32[]{:S(2)}, u32[]{:S(2)}) collective-permute-start(f32[4,8192]{1,0:T(4,128)S(1)} %slice.33), channel_id=1, source_target_pairs={{0,1},{1,0},{2,3},{3,2},{4,5},{5,4},{6,7},{7,6},{8,9},{9,8},{10,11... | collective-permute-start | bytes 393224 | tf_op jit(solution)/shard_map/ppermute | solution.py:226

commit v3 on v2

--- a/solution.py
+++ b/solution.py
@@ -10,6 +10,8 @@
 AXIS = "tensor"
 BLOCK = 64
 CHUNKS = 8
+PARTS = 8
+DOWN_PARTS = 2
 BF16 = jnp.bfloat16
 F32 = jnp.float32
 MIB = 2**20
@@ -46,45 +48,62 @@
     return (row == column // BLOCK).astype(BF16)
 
 
-def mask_kernel(flags_ref, *refs):
-    weights, masked, keeps, sems = refs[:3], refs[3:6], refs[6:9], refs[9]
-    copies = []
-    for index, (weight_ref, masked_ref) in enumerate(zip(weights, masked)):
-        rows = weight_ref.shape[0] // CHUNKS
-        for chunk in range(CHUNKS):
+def keep_lanes(flags, width, transposed):
+    return dot(flags, spread(width // BLOCK, width), 1 if transposed else 0, 0)
+
+
+class Weight:
+    def __init__(self, source, target, sems):
+        chunks = min(CHUNKS, source.shape[0] // BLOCK)
+        rows = source.shape[0] // chunks
+        self.target = target
+        self.copies = []
+        for chunk in range(chunks):
             at = pl.ds(chunk * rows, rows)
-            copies.append(
-                pltpu.make_async_copy(weight_ref.at[at, :], masked_ref.at[at, :], sems.at[index, chunk])
-            )
-    for copy in copies:
-        copy.start()
-    for index, (masked_ref, keep_ref) in enumerate(zip(masked, keeps)):
-        rows, columns = masked_ref.shape
-        flags = flags_ref[index].astype(F32).astype(BF16)
-        keep = dot(flags, spread(columns // BLOCK, columns), 0 if index == 2 else 1, 0)
+            self.copies.append(pltpu.make_async_copy(source.at[at, :], target.at[at, :], sems.at[chunk]))
+
+    def start(self):
+        for copy in self.copies:
+            copy.start()
+
+    def mask(self, keep):
+        keep = keep.astype(BF16)
+        blocks = self.target.shape[0] // BLOCK
+        each = blocks // len(self.copies)
+        for block in range(blocks):
+            if block % each == 0:
+                self.copies[block // each].wait()
+            at = pl.ds(block * BLOCK, BLOCK)
+            self.target[at, :] = self.target[at, :] * keep[block : block + 1, :]
+
+
+def mask_kernel(flags_ref, gate_hbm, up_hbm, down_hbm, after_ref, *refs):
+    targets, keeps, sems = refs[:3], refs[3:6], refs[6]
+    weights = [
+        Weight(source, target, sems.at[index])
+        for index, (source, target) in enumerate(zip((gate_hbm, up_hbm, down_hbm), targets))
+    ]
+    for weight in weights:
+        weight.start()
+    for index, (weight, keep_ref) in enumerate(zip(weights, keeps)):
+        keep = keep_lanes(flags_ref[index], keep_ref.shape[1], index == 2)
         keep_ref[...] = keep
-        keep = keep.astype(BF16)
-        blocks = rows // BLOCK
-        for block in range(blocks):
-            if block * CHUNKS % blocks == 0:
-                copies[index * CHUNKS + block * CHUNKS // blocks].wait()
-            at = pl.ds(block * BLOCK, BLOCK)
-            masked_ref[at, :] = masked_ref[at, :] * keep[block : block + 1, :]
-
-
-def mask_weights(flags, *weights):
+        weight.mask(keep)
+
+
+def mask_weights(flags, weights, after):
     hbm = pl.BlockSpec(memory_space=pltpu.HBM)
     return pl.pallas_call(
         mask_kernel,
         out_shape=tuple(pltpu.VMEM(w.shape, BF16) for w in weights)
         + tuple(shape(w.shape[0] // BLOCK, w.shape[1]) for w in weights),
-        in_specs=[VMEM] + [hbm] * 3,
+        in_specs=[VMEM] + [hbm] * 3 + [pl.BlockSpec(memory_space=pl.ANY)],
         out_specs=(VMEM,) * 6,
         scratch_shapes=[pltpu.SemaphoreType.DMA((3, CHUNKS))],
         compiler_params=params(8),
         cost_estimate=cost(0, sum(2 * w.size for w in weights)),
         name="mask",
-    )(flags, *map(in_hbm, weights))
+    )(flags, *map(in_hbm, weights), after)
 
 
 def layer_kernel(pieces, *refs):
@@ -147,56 +166,58 @@
 
 
 def grads_kernel(
-    tokens_ref, cotangent_ref, gate_delta_ref, up_delta_ref, hidden_t_ref, keep_g_ref, keep_u_ref, keep_d_ref,
-    gate_ref, up_ref, down_ref,
+    tokens_ref, cotangents_ref, gate_delta_ref, up_delta_ref, hidden_t_ref, keep_g_ref, keep_u_ref, keep_d_ref, after_ref,
+    gate_out, up_out, down_out, gate_ref, up_ref, down_ref, sems,
 ):
-    step = pl.program_id(0)
-    blocks = gate_ref.shape[0] // BLOCK
-    for delta_ref, keep_ref, out_ref in (
-        (gate_delta_ref, keep_g_ref, gate_ref),
-        (up_delta_ref, keep_u_ref, up_ref),
+    features, units = gate_ref.shape
+    copies = []
+
+    def send(ref, out, at):
+        copies.append(pltpu.make_async_copy(ref.at[at, :], out.at[at, :], sems.at[len(copies)]))
+        copies[-1].start()
+
+    def masked(grad, keep_ref, first, columns, out_ref):
+        for block in range(grad.shape[0] // BLOCK):
+            keep = keep_ref[first // BLOCK + block : first // BLOCK + block + 1, columns]
+            rows = grad[block * BLOCK : (block + 1) * BLOCK, :]
+            out_ref[pl.ds(first + block * BLOCK, BLOCK), columns] = (rows * keep).astype(BF16)
+
+    tall = features // PARTS
+    for delta_ref, keep_ref, ref, out in (
+        (gate_delta_ref, keep_g_ref, gate_ref, gate_out),
+        (up_delta_ref, keep_u_ref, up_ref, up_out),
     ):
-        grad = dot(tokens_ref[...], delta_ref[...], 0, 0)
-        for block in range(blocks):
-            keep = keep_ref[pl.ds(step * blocks + block, 1), :]
-            at = slice(block * BLOCK, (block + 1) * BLOCK)
-            out_ref[at, :] = (grad[at, :] * keep).astype(BF16)
-    grad = dot(hidden_t_ref[...], cotangent_ref[...])
-    down_ref[...] = (grad * keep_d_ref[pl.ds(step, 1), :]).astype(BF16)
-
-
-def grads(tokens, cotangents, gate_delta, up_delta, hidden_t, keeps):
+        for part in range(PARTS):
+            at = pl.ds(part * tall, tall)
+            masked(dot(tokens_ref[:, at], delta_ref[...], 0, 0), keep_ref, part * tall, pl.ds(0, units), ref)
+            send(ref, out, at)
+    flat = units // DOWN_PARTS
+    for part in range(DOWN_PARTS):
+        at = pl.ds(part * flat, flat)
+        for start in range(0, features, 512):
+            columns = pl.ds(start, 512)
+            masked(dot(hidden_t_ref[at, :], cotangents_ref[:, columns]), keep_d_ref, part * flat, columns, down_ref)
+        send(down_ref, down_out, at)
+    for copy in copies:
+        copy.wait()
+
+
+def grads(tokens, cotangents, gate_delta, up_delta, hidden_t, keeps, after):
     rows, features = tokens.shape
     units = hidden_t.shape[0]
-    steps = units // BLOCK
-    wide = features // steps
+    hbm = pl.BlockSpec(memory_space=pltpu.HBM)
+    shapes = ((features, units), (features, units), (units, features))
     return pl.pallas_call(
         grads_kernel,
-        grid=(steps,),
-        out_shape=(
-            shape(features, units, dtype=BF16),
-            shape(features, units, dtype=BF16),
-            shape(units, features, dtype=BF16),
-        ),
-        in_specs=[
-            pl.BlockSpec((rows, wide), lambda i: (0, i)),
-            VMEM,
-            VMEM,
-            VMEM,
-            pl.BlockSpec((BLOCK, rows), lambda i: (i, 0)),
-            VMEM,
-            VMEM,
-            VMEM,
-        ],
-        out_specs=(
-            pl.BlockSpec((wide, units), lambda i: (i, 0)),
-            pl.BlockSpec((wide, units), lambda i: (i, 0)),
-            pl.BlockSpec((BLOCK, features), lambda i: (i, 0)),
-        ),
-        compiler_params=params(16),
+        out_shape=tuple(shape(*dims, dtype=BF16) for dims in shapes),
+        in_specs=[VMEM] * 8 + [pl.BlockSpec(memory_space=pl.ANY)],
+        out_specs=(hbm,) * 3,
+        scratch_shapes=[pltpu.VMEM(dims, BF16) for dims in shapes]
+        + [pltpu.SemaphoreType.DMA((2 * PARTS + DOWN_PARTS,))],
+        compiler_params=params(30),
         cost_estimate=cost(6 * rows * features * units, 3 * 2 * features * units),
         name="grads",
-    )(tokens, cotangents, gate_delta, up_delta, hidden_t, *keeps)
+    )(tokens, cotangents, gate_delta, up_delta, hidden_t, *keeps, after)
 
 
 def across_cores(devices):
@@ -207,7 +228,10 @@
     def pairs(offsets):
         return [(i, ((i // 2) ^ offsets[i % 2]) * 2 + i % 2) for i in range(devices)]
 
-    return [pairs((k + 1, k) if k else (0, 1)) for k in range(0, devices // 2, 2)]
+    chips = devices // 2
+    offsets = [(k + 1, k) if k else (0, 1) for k in range(0, chips, 2)]
+    near = len(offsets) // 2
+    return [pairs(pair) for pair in offsets[:near] + offsets[:near - 1 : -1]]
 
 
 def gather(own, devices, after):
@@ -229,16 +253,19 @@
 def shards(devices, tokens, cotangent, gate_weight, up_weight, down_weight, block_mask):
     features = tokens.shape[1]
     cores = across_cores(devices)
-    own = jnp.concatenate(
-        [tokens, lax.ppermute(tokens, AXIS, cores), cotangent, lax.ppermute(cotangent, AXIS, cores)], 0
-    )
-    own, block_mask = lax.optimization_barrier((own, block_mask))
-    gate, up, down, *keeps = mask_weights(block_mask, gate_weight, up_weight, down_weight)
+    here = lax.optimization_barrier(jnp.concatenate([tokens, cotangent], 0))
+    flags = jnp.swapaxes(block_mask, 1, 2).astype(BF16)
+    other = lax.ppermute(tokens, AXIS, cores), lax.ppermute(cotangent, AXIS, cores)
+    here, flags, other = lax.optimization_barrier((here, flags, other))
+    rows = tokens.shape[0]
+    own = jnp.concatenate([here[:rows], other[0], here[rows:], other[1]], 0)
+    gate, up, down, *keeps = mask_weights(flags, (gate_weight, up_weight, down_weight), own)
     pieces, keeps[0] = gather(own, devices, keeps[0])
     all_tokens, all_cotangents, gate_delta, up_delta, hidden_t, mine, theirs = layer(pieces, gate, up, down)
     total = (mine + lax.ppermute(theirs, AXIS, cores).astype(F32)).astype(BF16)
-    total, hidden_t = lax.optimization_barrier((total, hidden_t))
-    gate_grad, up_grad, down_grad = grads(all_tokens, all_cotangents, gate_delta, up_delta, hidden_t, keeps)
+    gate_grad, up_grad, down_grad = grads(
+        all_tokens, all_cotangents, gate_delta, up_delta, hidden_t, keeps, total
+    )
     sums, down_grad = scatter(total, devices, down_grad)
     return sums[:, :features], sums[:, features:], gate_grad, up_grad, down_grad
 

time: 57.9 us -> 53.1 us (0.917)
  Pallas kernels: 32.7 us -> 29.3 us
  waiting for transfers between devices: 5.33 us -> 4.04 us
  local copies, waits for them, and re-layouts: 1.54 us -> 0.74 us
  other arithmetic: 1.04 us -> 1.82 us
    pallas_call x1, Pallas kernels: 12.5 us -> 9.08 us  [grads(): pl.pallas_call(grads_kernel, out_shape=tuple((shape(*dims, dtype=BF16) fo...]
    ppermute x1, waiting for transfers between devices: 0.99 us -> 0.01 us  [shards(): lax.ppermute(tokens, AXIS, cores)]
    optimization_barrier x1 -> x0, local copies, waits for them, and re-layouts: 0.83 us -> none  [shards(): own, block_mask = lax.optimization_barrier((own, block_mask))]
    convert_element_type x0 -> x1, other arithmetic: none -> 0.74 us  [shards(): flags = jnp.swapaxes(block_mask, 1, 2).astype(BF16)]
    ppermute x4, starting transfers between devices: 8.12 us -> 7.49 us  [gather(): mine = [lax.ppermute(own, AXIS, pairs) for pairs in across_chips(devices)]]
  transfers between devices with their start and end apart: 16 -> 16, of which waited for: 8 -> 6; matrix products, arithmetic and copies ran while one was open for 1% -> 3% of each run, Pallas kernels for 36% -> 33%
where the time goes in v3:
time: 53.1 us; the launch traced here: 52.9 us
  Pallas kernels  29.3 us (55%)
  starting transfers between devices  16.2 us (31%)
  waiting for transfers between devices  4.04 us (8%)
  other arithmetic  1.82 us (3%)
  between operations  0.79 us (1%)
  local copies, waits for them, and re-layouts  0.74 us (1%)
    pallas_call x1, Pallas kernels, layer(): pl.pallas_call(functools.partial(layer_kernel, len(pieces)), out_shape=(s...  11.7 us
    pallas_call x1, Pallas kernels, grads(): pl.pallas_call(grads_kernel, out_shape=tuple((shape(*dims, dtype=BF16) fo...  9.08 us
    pallas_call x1, Pallas kernels, mask_weights(): pl.pallas_call(mask_kernel, out_shape=tuple((pltpu.VMEM(w.shape, BF16) fo...  8.47 us
    ppermute x4, starting transfers between devices, gather(): mine = [lax.ppermute(own, AXIS, pairs) for pairs in across_chips(devices)]  7.49 us
    ppermute x4, starting transfers between devices, scatter(): lax.ppermute(total[k * rows:(k + 1) * rows], AXIS, pairs)  6 us
    ppermute x1, waiting for transfers between devices, shards(): total = (mine + lax.ppermute(theirs, AXIS, cores).astype(F32)).astype(BF16)  1.73 us
    ppermute x4, starting transfers between devices, gather(): lax.ppermute(piece, AXIS, across_cores(devices))  1.48 us
    ppermute x4, waiting for transfers between devices, gather(): lax.ppermute(piece, AXIS, across_cores(devices))  1.27 us
  transfers between devices with their start and end apart: 16, of which 6 were waited for; matrix products, arithmetic and copies ran while one was open for 3% of the time, Pallas kernels for 33%

profile of v3, /device:TPU:0, one launch (start us, length us, event | category | flops | bytes accessed | tf_op | source)
XLA Modules:
  0.0 52.9 jit_solution(7541313456512360257)
XLA Ops:
  0.6 0.5 collective-permute-start
  1.1 0.1 collective-permute-start.1
  1.2 0.8 %pad_maximum_fusion.1 = bf16[8,4096]{1,0:T(8,128)(2,1)S(1)} fusion(bf16[4,4096]{1,0:T(4,128)(2,1)} %param.7, bf16[4,4096]{1,0:T(4,128)(2,1)} %param.6), kind=kLoop, calls=%fused_computation.5 | loop fusion | flops 131072 | bytes 131072 | tf_op jit(solution)/shard_map/concatenate | solution.py:256
  2.0 0.7 %convert_bitcast_fusion.flags_ref = bf16[3,16,64]{2,1,0:T(8,128)(2,1)S(1)} fusion(s32[3,64,16]{1,2,0:T(8,128)} %param.11), kind=kLoop, calls=%fused_computation.6 | loop fusion | flops 3072 | bytes 18432 | tf_op jit(solution)/shard_map/convert_element_type | solution.py:257
  2.8 0.0 collective-permute-done
  2.8 0.0 collective-permute-done.1
  2.8 0.1 pad_maximum_fusion.after_ref
  2.9 5.0 %collective-permute-start.5 = (bf16[16,4096]{1,0:T(8,128)(2,1)S(1)}, bf16[16,4096]{1,0:T(8,128)(2,1)S(1)}, u32[]{:S(2)}, u32[]{:S(2)}) collective-permute-start(bf16[16,4096]{1,0:T(8,128)(2,1)S(1)} %pad_maximum_fusion.after_ref), channel_id=1, source_target_pairs={{0,10},{1,9},{2,8},{3,11},{4,14},{5,13},{6,12},{7,15},{8,2},{9,1},... | collective-permute-start | bytes 393224 | tf_op jit(solution)/shard_map/ppermute | solution.py:238
  8.0 1.3 %collective-permute-start.4 = (bf16[16,4096]{1,0:T(8,128)(2,1)S(1)}, bf16[16,4096]{1,0:T(8,128)(2,1)S(1)}, u32[]{:S(2)}, u32[]{:S(2)}) collective-permute-start(bf16[16,4096]{1,0:T(8,128)(2,1)S(1)} %pad_maximum_fusion.after_ref), channel_id=1, source_target_pairs={{0,14},{1,13},{2,12},{3,15},{4,10},{5,9},{6,8},{7,11},{8,6},{9,5},... | collective-permute-start | bytes 393224 | tf_op jit(solution)/shard_map/ppermute | solution.py:238
  9.2 0.5 collective-permute-start.3
  9.8 0.7 %collective-permute-start.2 = (bf16[16,4096]{1,0:T(8,128)(2,1)S(1)}, bf16[16,4096]{1,0:T(8,128)(2,1)S(1)}, u32[]{:S(2)}, u32[]{:S(2)}) collective-permute-start(bf16[16,4096]{1,0:T(8,128)(2,1)S(1)} %pad_maximum_fusion.after_ref), channel_id=1, source_target_pairs={{0,0},{1,3},{2,2},{3,1},{4,4},{5,7},{6,6},{7,5},{8,8},{9,11},{10,1... | collective-permute-start | bytes 393224 | tf_op jit(solution)/shard_map/ppermute | solution.py:238
  10.4 8.5 %mask.1 = (bf16[4096,1024]{1,0:T(8,128)(2,1)S(1)}, bf16[4096,1024]{1,0:T(8,128)(2,1)S(1)}, bf16[1024,4096]{1,0:T(8,128)(2,1)S(1)}, f32[64,1024]{1,0:T(8,128)S(1)...) custom-call(bf16[3,16,64]{2,1,0:T(8,128)(2,1)S(1)} %convert_bitcast_fusion.flags_ref, bf16[4096,1024]{1,0:T(8,128)(2,1)} %gate_hbm.1, ...), custom_call_target="tpu_custom_call" | custom-call | bytes 25165824 | tf_op jit(solution)/shard_map/mask/pallas_call | solution.py:96
  18.9 0.0 collective-permute-done.5.refs_3_
  18.9 0.0 collective-permute-done.4.refs_2_
  18.9 0.0 collective-permute-done.3.refs_1_
  18.9 0.0 collective-permute-done.2.refs_0_
  18.9 0.9 %collective-permute-start.6 = (bf16[16,4096]{1,0:T(8,128)(2,1)S(1)}, bf16[16,4096]{1,0:T(8,128)(2,1)S(1)}, u32[]{:S(2)}, u32[]{:S(2)}) collective-permute-start(bf16[16,4096]{1,0:T(8,128)(2,1)S(1)} %collective-permute-done.2.refs_0_), channel_id=1, source_target_pairs={{0,1},{1,0},{2,3},{3,2},{4,5},{5,4},{6,7},{7,6},{8,9},{9,8},{10,11... | collective-permute-start | bytes 393224 | tf_op jit(solution)/shard_map/ppermute | solution.py:240
  19.8 0.1 collective-permute-start.7
  19.9 0.4 collective-permute-start.8
  20.3 0.1 collective-permute-start.9
  20.4 0.4 collective-permute-done.6.refs_4_
  20.8 0.4 collective-permute-done.7.refs_5_
  21.2 0.2 collective-permute-done.8.refs_6_
  21.4 0.3 collective-permute-done.9.refs_7_
  21.7 11.7 %layer.1 = (bf16[64,4096]{1,0:T(8,128)(2,1)S(1)}, bf16[64,4096]{1,0:T(8,128)(2,1)S(1)}, bf16[64,1024]{1,0:T(8,128)(2,1)S(1)}, bf16[64,1024]{1,0:T(8,128)(2,1)S(1...) custom-call(bf16[16,4096]{1,0:T(8,128)(2,1)S(1)} %collective-permute-done.2.refs_0_, ...), custom_call_target="tpu_custom_call" | custom-call | flops 3221225472 | bytes 25165824 | tf_op jit(solution)/shard_map/layer/pallas_call | solution.py:148
  33.4 0.2 collective-permute-start.10
  33.6 1.7 %collective-permute-done.10 = bf16[32,8192]{1,0:T(8,128)(2,1)S(1)} collective-permute-done((bf16[32,8192]{1,0:T(8,128)(2,1)S(1)}, bf16[32,8192]{1,0:T(8,128)(2,1)S(1)}, u32[]{:S(2)}, u32[]{:S(2)}) %collective-permute-start.10) | collective-permute-done | bytes 524320 | tf_op jit(solution)/shard_map/ppermute | solution.py:265
  35.4 0.1 add_convert_fusion.after_ref
  35.5 3.1 %collective-permute-start.14 = (bf16[8,8192]{1,0:T(8,128)(2,1)S(1)}, bf16[8,8192]{1,0:T(8,128)(2,1)S(1)}, u32[]{:S(2)}, u32[]{:S(2)}) collective-permute-start(bf16[8,8192]{1,0:T(8,128)(2,1)S(1)} %get-tuple-element.65), channel_id=1, source_target_pairs={{0,10},{1,9},{2,8},{3,11},{4,14},{5,13},{6,12},{7,15},{8,2},{9,1},... | collective-permute-start | bytes 393224 | tf_op jit(solution)/shard_map/ppermute | solution.py:246
  38.6 2.0 %collective-permute-start.13 = (bf16[8,8192]{1,0:T(8,128)(2,1)S(1)}, bf16[8,8192]{1,0:T(8,128)(2,1)S(1)}, u32[]{:S(2)}, u32[]{:S(2)}) collective-permute-start(bf16[8,8192]{1,0:T(8,128)(2,1)S(1)} %get-tuple-element.66), channel_id=1, source_target_pairs={{0,14},{1,13},{2,12},{3,15},{4,10},{5,9},{6,8},{7,11},{8,6},{9,5},... | collective-permute-start | bytes 393224 | tf_op jit(solution)/shard_map/ppermute | solution.py:246
  40.7 0.0 collective-permute-start.12
  40.7 0.8 %collective-permute-start.11 = (bf16[8,8192]{1,0:T(8,128)(2,1)S(1)}, bf16[8,8192]{1,0:T(8,128)(2,1)S(1)}, u32[]{:S(2)}, u32[]{:S(2)}) collective-permute-start(bf16[8,8192]{1,0:T(8,128)(2,1)S(1)} %get-tuple-element.68), channel_id=1, source_target_pairs={{0,0},{1,3},{2,2},{3,1},{4,4},{5,7},{6,6},{7,5},{8,8},{9,11},{10,1... | collective-permute-start | bytes 393224 | tf_op jit(solution)/shard_map/ppermute | solution.py:246
  41.5 9.1 %grads.1 = (bf16[4096,1024]{1,0:T(8,128)(2,1)}, bf16[4096,1024]{1,0:T(8,128)(2,1)}, bf16[1024,4096]{1,0:T(8,128)(2,1)}) custom-call(bf16[64,4096]{1,0:T(8,128)(2,1)S(1)} %get-tuple-element.49.tokens_ref, bf16[64,4096]{1,0:T(8,128)(2,1)S(1)} %get-tuple-element.50.cotangents_ref, bf16[64,1024]{1,0:T(8,128)(2,1)S(1)} %get-tuple-element.51.gate_delta_ref, ...), custom_call_target="tpu_custom_call" | custom-call | flops 1610612736 | bytes 25165824 | tf_op jit(solution)/shard_map/grads/pallas_call | solution.py:210
  50.6 0.0 collective-permute-done.14
  50.6 0.0 collective-permute-done.13
  50.6 0.0 collective-permute-done.12
  50.6 0.0 collective-permute-done.11
  50.7 0.1 convert_add_fusion
  50.8 0.4 collective-permute-start.15
  51.2 1.0 %collective-permute-done.15 = f32[4,8192]{1,0:T(4,128)S(1)} collective-permute-done((f32[4,8192]{1,0:T(4,128)S(1)}, f32[4,8192]{1,0:T(4,128)S(1)}, u32[]{:S(2)}, u32[]{:S(2)}) %collective-permute-start.15) | collective-permute-done | bytes 131104 | tf_op jit(solution)/shard_map/ppermute | solution.py:250
  52.2 0.7 %fusion.2 = (bf16[4,4096]{1,0:T(4,128)(2,1)}, bf16[4,4096]{1,0:T(4,128)(2,1)}) fusion(bf16[4,8192]{1,0:T(4,128)(2,1)S(1)} %fusion), kind=kLoop, calls=%fused_computation.8 | loop fusion | bytes 131072 | tf_op jit(solution)/shard_map/slice | solution.py:270
  (4 shorter events, 0.1 us)
Async XLA Ops:
  0.6 2.2 %collective-permute-start = (bf16[4,4096]{1,0:T(4,128)(2,1)}, bf16[4,4096]{1,0:T(4,128)(2,1)S(1)}, u32[]{:S(2)}, u32[]{:S(2)}) collective-permute-start(bf16[4,4096]{1,0:T(4,128)(2,1)} %param.6), channel_id=1, source_target_pairs={{0,1},{1,0},{2,3},{3,2},{4,5},{5,4},{6,7},{7,6},{8,9},{9,8},{10,11... | collective-permute-start | bytes 98312 | tf_op jit(solution)/shard_map/ppermute | solution.py:258
  1.1 1.6 %collective-permute-start.1 = (bf16[4,4096]{1,0:T(4,128)(2,1)}, bf16[4,4096]{1,0:T(4,128)(2,1)S(1)}, u32[]{:S(2)}, u32[]{:S(2)}) collective-permute-start(bf16[4,4096]{1,0:T(4,128)(2,1)} %param.7), channel_id=1, source_target_pairs={{0,1},{1,0},{2,3},{3,2},{4,5},{5,4},{6,7},{7,6},{8,9},{9,8},{10,11... | collective-permute-start | bytes 98312 | tf_op jit(solution)/shard_map/ppermute | solution.py:258
  2.9 16.0 %collective-permute-start.5 = (bf16[16,4096]{1,0:T(8,128)(2,1)S(1)}, bf16[16,4096]{1,0:T(8,128)(2,1)S(1)}, u32[]{:S(2)}, u32[]{:S(2)}) collective-permute-start(bf16[16,4096]{1,0:T(8,128)(2,1)S(1)} %pad_maximum_fusion.after_ref), channel_id=1, source_target_pairs={{0,10},{1,9},{2,8},{3,11},{4,14},{5,13},{6,12},{7,15},{8,2},{9,1},... | collective-permute-start | bytes 393224 | tf_op jit(solution)/shard_map/ppermute | solution.py:238
  8.0 11.0 %collective-permute-start.4 = (bf16[16,4096]{1,0:T(8,128)(2,1)S(1)}, bf16[16,4096]{1,0:T(8,128)(2,1)S(1)}, u32[]{:S(2)}, u32[]{:S(2)}) collective-permute-start(bf16[16,4096]{1,0:T(8,128)(2,1)S(1)} %pad_maximum_fusion.after_ref), channel_id=1, source_target_pairs={{0,14},{1,13},{2,12},{3,15},{4,10},{5,9},{6,8},{7,11},{8,6},{9,5},... | collective-permute-start | bytes 393224 | tf_op jit(solution)/shard_map/ppermute | solution.py:238
  9.2 9.7 %collective-permute-start.3 = (bf16[16,4096]{1,0:T(8,128)(2,1)S(1)}, bf16[16,4096]{1,0:T(8,128)(2,1)S(1)}, u32[]{:S(2)}, u32[]{:S(2)}) collective-permute-start(bf16[16,4096]{1,0:T(8,128)(2,1)S(1)} %pad_maximum_fusion.after_ref), channel_id=1, source_target_pairs={{0,6},{1,5},{2,4},{3,7},{4,2},{5,1},{6,0},{7,3},{8,14},{9,13},{10,... | collective-permute-start | bytes 393224 | tf_op jit(solution)/shard_map/ppermute | solution.py:238
  9.8 9.2 %collective-permute-start.2 = (bf16[16,4096]{1,0:T(8,128)(2,1)S(1)}, bf16[16,4096]{1,0:T(8,128)(2,1)S(1)}, u32[]{:S(2)}, u32[]{:S(2)}) collective-permute-start(bf16[16,4096]{1,0:T(8,128)(2,1)S(1)} %pad_maximum_fusion.after_ref), channel_id=1, source_target_pairs={{0,0},{1,3},{2,2},{3,1},{4,4},{5,7},{6,6},{7,5},{8,8},{9,11},{10,1... | collective-permute-start | bytes 393224 | tf_op jit(solution)/shard_map/ppermute | solution.py:238
  18.9 1.9 %collective-permute-start.6 = (bf16[16,4096]{1,0:T(8,128)(2,1)S(1)}, bf16[16,4096]{1,0:T(8,128)(2,1)S(1)}, u32[]{:S(2)}, u32[]{:S(2)}) collective-permute-start(bf16[16,4096]{1,0:T(8,128)(2,1)S(1)} %collective-permute-done.2.refs_0_), channel_id=1, source_target_pairs={{0,1},{1,0},{2,3},{3,2},{4,5},{5,4},{6,7},{7,6},{8,9},{9,8},{10,11... | collective-permute-start | bytes 393224 | tf_op jit(solution)/shard_map/ppermute | solution.py:240
  19.8 1.3 %collective-permute-start.7 = (bf16[16,4096]{1,0:T(8,128)(2,1)S(1)}, bf16[16,4096]{1,0:T(8,128)(2,1)S(1)}, u32[]{:S(2)}, u32[]{:S(2)}) collective-permute-start(bf16[16,4096]{1,0:T(8,128)(2,1)S(1)} %collective-permute-done.3.refs_1_), channel_id=1, source_target_pairs={{0,1},{1,0},{2,3},{3,2},{4,5},{5,4},{6,7},{7,6},{8,9},{9,8},{10,11... | collective-permute-start | bytes 393224 | tf_op jit(solution)/shard_map/ppermute | solution.py:240
  19.9 1.5 %collective-permute-start.8 = (bf16[16,4096]{1,0:T(8,128)(2,1)S(1)}, bf16[16,4096]{1,0:T(8,128)(2,1)S(1)}, u32[]{:S(2)}, u32[]{:S(2)}) collective-permute-start(bf16[16,4096]{1,0:T(8,128)(2,1)S(1)} %collective-permute-done.4.refs_2_), channel_id=1, source_target_pairs={{0,1},{1,0},{2,3},{3,2},{4,5},{5,4},{6,7},{7,6},{8,9},{9,8},{10,11... | collective-permute-start | bytes 393224 | tf_op jit(solution)/shard_map/ppermute | solution.py:240
  20.3 1.3 %collective-permute-start.9 = (bf16[16,4096]{1,0:T(8,128)(2,1)S(1)}, bf16[16,4096]{1,0:T(8,128)(2,1)S(1)}, u32[]{:S(2)}, u32[]{:S(2)}) collective-permute-start(bf16[16,4096]{1,0:T(8,128)(2,1)S(1)} %collective-permute-done.5.refs_3_), channel_id=1, source_target_pairs={{0,1},{1,0},{2,3},{3,2},{4,5},{5,4},{6,7},{7,6},{8,9},{9,8},{10,11... | collective-permute-start | bytes 393224 | tf_op jit(solution)/shard_map/ppermute | solution.py:240
  33.4 2.0 %collective-permute-start.10 = (bf16[32,8192]{1,0:T(8,128)(2,1)S(1)}, bf16[32,8192]{1,0:T(8,128)(2,1)S(1)}, u32[]{:S(2)}, u32[]{:S(2)}) collective-permute-start(bf16[32,8192]{1,0:T(8,128)(2,1)S(1)} %get-tuple-element.48), channel_id=1, source_target_pairs={{0,1},{1,0},{2,3},{3,2},{4,5},{5,4},{6,7},{7,6},{8,9},{9,8},{10,11... | collective-permute-start | bytes 1572872 | tf_op jit(solution)/shard_map/ppermute | solution.py:265
  35.5 15.1 %collective-permute-start.14 = (bf16[8,8192]{1,0:T(8,128)(2,1)S(1)}, bf16[8,8192]{1,0:T(8,128)(2,1)S(1)}, u32[]{:S(2)}, u32[]{:S(2)}) collective-permute-start(bf16[8,8192]{1,0:T(8,128)(2,1)S(1)} %get-tuple-element.65), channel_id=1, source_target_pairs={{0,10},{1,9},{2,8},{3,11},{4,14},{5,13},{6,12},{7,15},{8,2},{9,1},... | collective-permute-start | bytes 393224 | tf_op jit(solution)/shard_map/ppermute | solution.py:246
  38.6 12.0 %collective-permute-start.13 = (bf16[8,8192]{1,0:T(8,128)(2,1)S(1)}, bf16[8,8192]{1,0:T(8,128)(2,1)S(1)}, u32[]{:S(2)}, u32[]{:S(2)}) collective-permute-start(bf16[8,8192]{1,0:T(8,128)(2,1)S(1)} %get-tuple-element.66), channel_id=1, source_target_pairs={{0,14},{1,13},{2,12},{3,15},{4,10},{5,9},{6,8},{7,11},{8,6},{9,5},... | collective-permute-start | bytes 393224 | tf_op jit(solution)/shard_map/ppermute | solution.py:246
  40.7 10.0 %collective-permute-start.12 = (bf16[8,8192]{1,0:T(8,128)(2,1)S(1)}, bf16[8,8192]{1,0:T(8,128)(2,1)S(1)}, u32[]{:S(2)}, u32[]{:S(2)}) collective-permute-start(bf16[8,8192]{1,0:T(8,128)(2,1)S(1)} %get-tuple-element.67), channel_id=1, source_target_pairs={{0,6},{1,5},{2,4},{3,7},{4,2},{5,1},{6,0},{7,3},{8,14},{9,13},{10,... | collective-permute-start | bytes 393224 | tf_op jit(solution)/shard_map/ppermute | solution.py:246
  40.7 10.0 %collective-permute-start.11 = (bf16[8,8192]{1,0:T(8,128)(2,1)S(1)}, bf16[8,8192]{1,0:T(8,128)(2,1)S(1)}, u32[]{:S(2)}, u32[]{:S(2)}) collective-permute-start(bf16[8,8192]{1,0:T(8,128)(2,1)S(1)} %get-tuple-element.68), channel_id=1, source_target_pairs={{0,0},{1,3},{2,2},{3,1},{4,4},{5,7},{6,6},{7,5},{8,8},{9,11},{10,1... | collective-permute-start | bytes 393224 | tf_op jit(solution)/shard_map/ppermute | solution.py:246
  50.8 1.4 %collective-permute-start.15 = (f32[4,8192]{1,0:T(4,128)S(1)}, f32[4,8192]{1,0:T(4,128)S(1)}, u32[]{:S(2)}, u32[]{:S(2)}) collective-permute-start(f32[4,8192]{1,0:T(4,128)S(1)} %slice.45), channel_id=1, source_target_pairs={{0,1},{1,0},{2,3},{3,2},{4,5},{5,4},{6,7},{7,6},{8,9},{9,8},{10,11... | collective-permute-start | bytes 393224 | tf_op jit(solution)/shard_map/ppermute | solution.py:250

commit v4 on v3

--- a/solution.py
+++ b/solution.py
@@ -11,7 +11,7 @@
 BLOCK = 64
 CHUNKS = 8
 PARTS = 8
-DOWN_PARTS = 2
+SLOTS = 10
 BF16 = jnp.bfloat16
 F32 = jnp.float32
 MIB = 2**20
@@ -66,7 +66,7 @@
         for copy in self.copies:
             copy.start()
 
-    def mask(self, keep):
+    def mask(self, keep, transposed=None):
         keep = keep.astype(BF16)
         blocks = self.target.shape[0] // BLOCK
         each = blocks // len(self.copies)
@@ -75,10 +75,13 @@
                 self.copies[block // each].wait()
             at = pl.ds(block * BLOCK, BLOCK)
             self.target[at, :] = self.target[at, :] * keep[block : block + 1, :]
+            if transposed is not None and block % 2:
+                pair = pl.ds((block - 1) * BLOCK, 2 * BLOCK)
+                transposed[:, pair] = self.target[pair, :].T
 
 
 def mask_kernel(flags_ref, gate_hbm, up_hbm, down_hbm, after_ref, *refs):
-    targets, keeps, sems = refs[:3], refs[3:6], refs[6]
+    targets, transposed, keeps, sems = refs[:3], (*refs[3:5], None), refs[5:8], refs[8]
     weights = [
         Weight(source, target, sems.at[index])
         for index, (source, target) in enumerate(zip((gate_hbm, up_hbm, down_hbm), targets))
@@ -88,7 +91,7 @@
     for index, (weight, keep_ref) in enumerate(zip(weights, keeps)):
         keep = keep_lanes(flags_ref[index], keep_ref.shape[1], index == 2)
         keep_ref[...] = keep
-        weight.mask(keep)
+        weight.mask(keep, transposed[index])
 
 
 def mask_weights(flags, weights, after):
@@ -96,9 +99,10 @@
     return pl.pallas_call(
         mask_kernel,
         out_shape=tuple(pltpu.VMEM(w.shape, BF16) for w in weights)
+        + tuple(pltpu.VMEM(w.shape[::-1], BF16) for w in weights[:2])
         + tuple(shape(w.shape[0] // BLOCK, w.shape[1]) for w in weights),
         in_specs=[VMEM] + [hbm] * 3 + [pl.BlockSpec(memory_space=pl.ANY)],
-        out_specs=(VMEM,) * 6,
+        out_specs=(VMEM,) * 8,
         scratch_shapes=[pltpu.SemaphoreType.DMA((3, CHUNKS))],
         compiler_params=params(8),
         cost_estimate=cost(0, sum(2 * w.size for w in weights)),
@@ -108,11 +112,11 @@
 
 def layer_kernel(pieces, *refs):
     piece_refs = refs[:pieces]
-    gate_ref, up_ref, down_ref = refs[pieces : pieces + 3]
+    gate_ref, up_ref, down_ref, gate_t_ref, up_t_ref = refs[pieces : pieces + 5]
     tokens_ref, cotangents_ref, gate_delta_ref, up_delta_ref, hidden_t_ref, mine_ref, theirs_ref = refs[
-        pieces + 3 : pieces + 10
+        pieces + 5 : pieces + 12
     ]
-    hidden_ref = refs[pieces + 10]
+    hidden_ref = refs[pieces + 12]
     features, units = gate_ref.shape
     both = [piece[...] for piece in piece_refs]
     tokens_ref[...] = jnp.concatenate([piece[: piece.shape[0] // 2] for piece in both], 0)
@@ -135,14 +139,14 @@
         mixed = dot(hidden_ref[...], down_ref[:, at])
         mine_ref[:, at] = mixed[:half]
         theirs_ref[:, at] = mixed[half:].astype(BF16)
-        grad = dot(gate_delta_ref[...], gate_ref[at, :], 1, 1)
-        grad += dot(up_delta_ref[...], up_ref[at, :], 1, 1)
+        grad = dot(gate_delta_ref[...], gate_t_ref[:, at])
+        grad += dot(up_delta_ref[...], up_t_ref[:, at])
         at = pl.ds(features + start, 512)
         mine_ref[:, at] = grad[:half]
         theirs_ref[:, at] = grad[half:].astype(BF16)
 
 
-def layer(pieces, gate, up, down):
+def layer(pieces, gate, up, down, gate_t, up_t):
     rows = sum(piece.shape[0] for piece in pieces) // 2
     features, units = gate.shape
     return pl.pallas_call(
@@ -156,55 +160,66 @@
             shape(rows // 2, 2 * features),
             shape(rows // 2, 2 * features, dtype=BF16),
         ),
-        in_specs=[VMEM] * (len(pieces) + 3),
+        in_specs=[VMEM] * (len(pieces) + 5),
         out_specs=(VMEM,) * 7,
         scratch_shapes=[pltpu.VMEM((rows, units), BF16)],
-        compiler_params=params(16),
+        compiler_params=params(8),
         cost_estimate=cost(12 * rows * features * units, 3 * 2 * features * units),
         name="layer",
-    )(*pieces, *map(in_vmem, (gate, up, down)))
+    )(*pieces, *map(in_vmem, (gate, up, down, gate_t, up_t)))
 
 
 def grads_kernel(
     tokens_ref, cotangents_ref, gate_delta_ref, up_delta_ref, hidden_t_ref, keep_g_ref, keep_u_ref, keep_d_ref, after_ref,
-    gate_out, up_out, down_out, gate_ref, up_ref, down_ref, sems,
+    gate_out, up_out, down_out, ring_ref, sems,
 ):
-    features, units = gate_ref.shape
+    features, units = gate_out.shape
+    slots, tall, _ = ring_ref.shape
     copies = []
 
-    def send(ref, out, at):
-        copies.append(pltpu.make_async_copy(ref.at[at, :], out.at[at, :], sems.at[len(copies)]))
+    def slot(rows):
+        count = len(copies)
+        if count >= slots and count % 2 == 0:
+            copies[count - slots].wait()
+            copies[count - slots + 1].wait()
+        return ring_ref.at[count % slots, pl.ds(0, rows), :]
+
+    def fill(part_ref, columns, grad, keep):
+        for block in range(grad.shape[0] // BLOCK):
+            at = slice(block * BLOCK, (block + 1) * BLOCK)
+            part_ref[at, columns] = (grad[at, :] * keep[block : block + 1, :]).astype(BF16)
+
+    def send(part_ref, out):
+        copies.append(pltpu.make_async_copy(part_ref, out, sems.at[len(copies)]))
         copies[-1].start()
 
-    def masked(grad, keep_ref, first, columns, out_ref):
-        for block in range(grad.shape[0] // BLOCK):
-            keep = keep_ref[first // BLOCK + block : first // BLOCK + block + 1, columns]
-            rows = grad[block * BLOCK : (block + 1) * BLOCK, :]
-            out_ref[pl.ds(first + block * BLOCK, BLOCK), columns] = (rows * keep).astype(BF16)
-
-    tall = features // PARTS
-    for delta_ref, keep_ref, ref, out in (
-        (gate_delta_ref, keep_g_ref, gate_ref, gate_out),
-        (up_delta_ref, keep_u_ref, up_ref, up_out),
-    ):
-        for part in range(PARTS):
-            at = pl.ds(part * tall, tall)
-            masked(dot(tokens_ref[:, at], delta_ref[...], 0, 0), keep_ref, part * tall, pl.ds(0, units), ref)
-            send(ref, out, at)
-    flat = units // DOWN_PARTS
-    for part in range(DOWN_PARTS):
-        at = pl.ds(part * flat, flat)
-        for start in range(0, features, 512):
-            columns = pl.ds(start, 512)
-            masked(dot(hidden_t_ref[at, :], cotangents_ref[:, columns]), keep_d_ref, part * flat, columns, down_ref)
-        send(down_ref, down_out, at)
-    for copy in copies:
+    for delta_ref, keep_ref, out in ((gate_delta_ref, keep_g_ref, gate_out), (up_delta_ref, keep_u_ref, up_out)):
+        for first in range(0, features, tall):
+            at = pl.ds(first, tall)
+            part_ref = slot(tall)
+            grad = dot(tokens_ref[:, at], delta_ref[...], 0, 0)
+            fill(part_ref, slice(0, units), grad, keep_ref[pl.ds(first // BLOCK, tall // BLOCK), :])
+            send(part_ref, out.at[at, :])
+    flat = min(tall, units)
+    wide = min(512, units)
+    for first in range(0, units, flat):
+        at = pl.ds(first, flat)
+        for left in range(0, features, units):
+            part_ref = slot(flat)
+            for start in range(0, units, wide):
+                columns = pl.ds(left + start, wide)
+                grad = dot(hidden_t_ref[at, :], cotangents_ref[:, columns])
+                keep = keep_d_ref[pl.ds(first // BLOCK, flat // BLOCK), columns]
+                fill(part_ref, slice(start, start + wide), grad, keep)
+            send(part_ref, down_out.at[at, pl.ds(left, units)])
+    for copy in copies[-slots:]:
         copy.wait()
 
 
 def grads(tokens, cotangents, gate_delta, up_delta, hidden_t, keeps, after):
     rows, features = tokens.shape
     units = hidden_t.shape[0]
+    tall = features // PARTS
     hbm = pl.BlockSpec(memory_space=pltpu.HBM)
     shapes = ((features, units), (features, units), (units, features))
     return pl.pallas_call(
@@ -212,9 +227,11 @@
         out_shape=tuple(shape(*dims, dtype=BF16) for dims in shapes),
         in_specs=[VMEM] * 8 + [pl.BlockSpec(memory_space=pl.ANY)],
         out_specs=(hbm,) * 3,
-        scratch_shapes=[pltpu.VMEM(dims, BF16) for dims in shapes]
-        + [pltpu.SemaphoreType.DMA((2 * PARTS + DOWN_PARTS,))],
-        compiler_params=params(30),
+        scratch_shapes=[
+            pltpu.VMEM((SLOTS, tall, units), BF16),
+            pltpu.SemaphoreType.DMA((2 * PARTS + features // min(tall, units),)),
+        ],
+        compiler_params=params(11),
         cost_estimate=cost(6 * rows * features * units, 3 * 2 * features * units),
         name="grads",
     )(tokens, cotangents, gate_delta, up_delta, hidden_t, *keeps, after)
@@ -259,9 +276,11 @@
     here, flags, other = lax.optimization_barrier((here, flags, other))
     rows = tokens.shape[0]
     own = jnp.concatenate([here[:rows], other[0], here[rows:], other[1]], 0)
-    gate, up, down, *keeps = mask_weights(flags, (gate_weight, up_weight, down_weight), own)
+    gate, up, down, gate_t, up_t, *keeps = mask_weights(flags, (gate_weight, up_weight, down_weight), own)
     pieces, keeps[0] = gather(own, devices, keeps[0])
-    all_tokens, all_cotangents, gate_delta, up_delta, hidden_t, mine, theirs = layer(pieces, gate, up, down)
+    all_tokens, all_cotangents, gate_delta, up_delta, hidden_t, mine, theirs = layer(
+        pieces, gate, up, down, gate_t, up_t
+    )
     total = (mine + lax.ppermute(theirs, AXIS, cores).astype(F32)).astype(BF16)
     gate_grad, up_grad, down_grad = grads(
         all_tokens, all_cotangents, gate_delta, up_delta, hidden_t, keeps, total

time: 53.1 us -> 51.5 us (0.970)
  Pallas kernels: 29.3 us -> 27.7 us
    pallas_call x1, Pallas kernels: 11.7 us -> 9.87 us  [layer(): pl.pallas_call(functools.partial(layer_kernel, len(pieces)), out_shape=(s...]
  transfers between devices with their start and end apart: 16 -> 16, of which waited for: 6 -> 6; matrix products, arithmetic and copies ran while one was open for 3% -> 3% of each run, Pallas kernels for 33% -> 35%
where the time goes in v4:
time: 51.5 us; the launch traced here: 51.2 us
  Pallas kernels  27.7 us (54%)
  starting transfers between devices  16 us (31%)
  waiting for transfers between devices  4.03 us (8%)
  other arithmetic  1.87 us (4%)
  between operations  0.79 us (2%)
  local copies, waits for them, and re-layouts  0.74 us (1%)
    pallas_call x1, Pallas kernels, layer(): pl.pallas_call(functools.partial(layer_kernel, len(pieces)), out_shape=(s...  9.87 us
    pallas_call x1, Pallas kernels, grads(): pl.pallas_call(grads_kernel, out_shape=tuple((shape(*dims, dtype=BF16) fo...  9.13 us
    pallas_call x1, Pallas kernels, mask_weights(): pl.pallas_call(mask_kernel, out_shape=tuple((pltpu.VMEM(w.shape, BF16) fo...  8.75 us
    ppermute x4, starting transfers between devices, gather(): mine = [lax.ppermute(own, AXIS, pairs) for pairs in across_chips(devices)]  7.49 us
    ppermute x4, starting transfers between devices, scatter(): lax.ppermute(total[k * rows:(k + 1) * rows], AXIS, pairs)  5.82 us
    ppermute x1, waiting for transfers between devices, shards(): total = (mine + lax.ppermute(theirs, AXIS, cores).astype(F32)).astype(BF16)  1.72 us
    ppermute x4, starting transfers between devices, gather(): lax.ppermute(piece, AXIS, across_cores(devices))  1.48 us
    ppermute x4, waiting for transfers between devices, gather(): lax.ppermute(piece, AXIS, across_cores(devices))  1.27 us
  transfers between devices with their start and end apart: 16, of which 6 were waited for; matrix products, arithmetic and copies ran while one was open for 3% of the time, Pallas kernels for 35%

profile of v4, /device:TPU:0, one launch (start us, length us, event | category | flops | bytes accessed | tf_op | source)
XLA Modules:
  0.0 51.2 jit_solution(3996999812491330385)
XLA Ops:
  0.6 0.5 %collective-permute-start = (bf16[4,4096]{1,0:T(4,128)(2,1)}, bf16[4,4096]{1,0:T(4,128)(2,1)S(1)}, u32[]{:S(2)}, u32[]{:S(2)}) collective-permute-start(bf16[4,4096]{1,0:T(4,128)(2,1)} %param.6), channel_id=1, source_target_pairs={{0,1},{1,0},{2,3},{3,2},{4,5},{5,4},{6,7},{7,6},{8,9},{9,8},{10,11... | collective-permute-start | bytes 98312 | tf_op jit(solution)/shard_map/ppermute | solution.py:275
  1.1 0.1 collective-permute-start.1
  1.2 0.8 %pad_maximum_fusion.1 = bf16[8,4096]{1,0:T(8,128)(2,1)S(1)} fusion(bf16[4,4096]{1,0:T(4,128)(2,1)} %param.7, bf16[4,4096]{1,0:T(4,128)(2,1)} %param.6), kind=kLoop, calls=%fused_computation.5 | loop fusion | flops 131072 | bytes 131072 | tf_op jit(solution)/shard_map/concatenate | solution.py:273
  2.0 0.7 %convert_bitcast_fusion.flags_ref = bf16[3,16,64]{2,1,0:T(8,128)(2,1)S(1)} fusion(s32[3,64,16]{1,2,0:T(8,128)} %param.11), kind=kLoop, calls=%fused_computation.6 | loop fusion | flops 3072 | bytes 18432 | tf_op jit(solution)/shard_map/convert_element_type | solution.py:274
  2.8 0.0 collective-permute-done
  2.8 0.0 collective-permute-done.1
  2.8 0.1 pad_maximum_fusion.after_ref
  2.9 5.0 %collective-permute-start.5 = (bf16[16,4096]{1,0:T(8,128)(2,1)S(1)}, bf16[16,4096]{1,0:T(8,128)(2,1)S(1)}, u32[]{:S(2)}, u32[]{:S(2)}) collective-permute-start(bf16[16,4096]{1,0:T(8,128)(2,1)S(1)} %pad_maximum_fusion.after_ref), channel_id=1, source_target_pairs={{0,10},{1,9},{2,8},{3,11},{4,14},{5,13},{6,12},{7,15},{8,2},{9,1},... | collective-permute-start | bytes 393224 | tf_op jit(solution)/shard_map/ppermute | solution.py:255
  8.0 1.3 %collective-permute-start.4 = (bf16[16,4096]{1,0:T(8,128)(2,1)S(1)}, bf16[16,4096]{1,0:T(8,128)(2,1)S(1)}, u32[]{:S(2)}, u32[]{:S(2)}) collective-permute-start(bf16[16,4096]{1,0:T(8,128)(2,1)S(1)} %pad_maximum_fusion.after_ref), channel_id=1, source_target_pairs={{0,14},{1,13},{2,12},{3,15},{4,10},{5,9},{6,8},{7,11},{8,6},{9,5},... | collective-permute-start | bytes 393224 | tf_op jit(solution)/shard_map/ppermute | solution.py:255
  9.2 0.5 collective-permute-start.3
  9.8 0.7 %collective-permute-start.2 = (bf16[16,4096]{1,0:T(8,128)(2,1)S(1)}, bf16[16,4096]{1,0:T(8,128)(2,1)S(1)}, u32[]{:S(2)}, u32[]{:S(2)}) collective-permute-start(bf16[16,4096]{1,0:T(8,128)(2,1)S(1)} %pad_maximum_fusion.after_ref), channel_id=1, source_target_pairs={{0,0},{1,3},{2,2},{3,1},{4,4},{5,7},{6,6},{7,5},{8,8},{9,11},{10,1... | collective-permute-start | bytes 393224 | tf_op jit(solution)/shard_map/ppermute | solution.py:255
  10.4 8.7 %mask.1 = (bf16[4096,1024]{1,0:T(8,128)(2,1)S(1)}, bf16[4096,1024]{1,0:T(8,128)(2,1)S(1)}, bf16[1024,4096]{1,0:T(8,128)(2,1)S(1)}, bf16[1024,4096]{1,0:T(8,128)(...) custom-call(bf16[3,16,64]{2,1,0:T(8,128)(2,1)S(1)} %convert_bitcast_, ...), custom_call_target="tpu_custom_call" | custom-call | bytes 25165824 | tf_op jit(solution)/shard_map/mask/pallas_call | solution.py:99
  19.2 0.0 collective-permute-done.5.refs_3_
  19.2 0.0 collective-permute-done.4.refs_2_
  19.2 0.0 collective-permute-done.3.refs_1_
  19.2 0.0 collective-permute-done.2.refs_0_
  19.2 0.9 %collective-permute-start.6 = (bf16[16,4096]{1,0:T(8,128)(2,1)S(1)}, bf16[16,4096]{1,0:T(8,128)(2,1)S(1)}, u32[]{:S(2)}, u32[]{:S(2)}) collective-permute-start(bf16[16,4096]{1,0:T(8,128)(2,1)S(1)} %collective-permute-done.2.refs_0_), channel_id=1, source_target_pairs={{0,1},{1,0},{2,3},{3,2},{4,5},{5,4},{6,7},{7,6},{8,9},{9,8},{10,11... | collective-permute-start | bytes 393224 | tf_op jit(solution)/shard_map/ppermute | solution.py:257
  20.1 0.1 collective-permute-start.7
  20.2 0.4 collective-permute-start.8
  20.6 0.1 collective-permute-start.9
  20.7 0.4 collective-permute-done.6.refs_4_
  21.1 0.4 collective-permute-done.7.refs_5_
  21.5 0.2 collective-permute-done.8.refs_6_
  21.6 0.3 collective-permute-done.9.refs_7_
  22.0 9.9 %layer.1 = (bf16[64,4096]{1,0:T(8,128)(2,1)S(1)}, bf16[64,4096]{1,0:T(8,128)(2,1)S(1)}, bf16[64,1024]{1,0:T(8,128)(2,1)S(1)}, bf16[64,1024]{1,0:T(8,128)(2,1)S(1...) custom-call(bf16[16,4096]{1,0:T(8,128)(2,1)S(1)} %collective-permute-done.2.refs_0_, ...), custom_call_target="tpu_custom_call" | custom-call | flops 3221225472 | bytes 25165824 | tf_op jit(solution)/shard_map/layer/pallas_call | solution.py:152
  31.8 0.3 collective-permute-start.10
  32.1 1.7 %collective-permute-done.10 = bf16[32,8192]{1,0:T(8,128)(2,1)S(1)} collective-permute-done((bf16[32,8192]{1,0:T(8,128)(2,1)S(1)}, bf16[32,8192]{1,0:T(8,128)(2,1)S(1)}, u32[]{:S(2)}, u32[]{:S(2)}) %collective-permute-start.10) | collective-permute-done | bytes 524320 | tf_op jit(solution)/shard_map/ppermute | solution.py:284
  33.8 0.1 add_convert_fusion.after_ref
  34.0 2.9 %collective-permute-start.14 = (bf16[8,8192]{1,0:T(8,128)(2,1)S(1)}, bf16[8,8192]{1,0:T(8,128)(2,1)S(1)}, u32[]{:S(2)}, u32[]{:S(2)}) collective-permute-start(bf16[8,8192]{1,0:T(8,128)(2,1)S(1)} %get-tuple-element.69), channel_id=1, source_target_pairs={{0,10},{1,9},{2,8},{3,11},{4,14},{5,13},{6,12},{7,15},{8,2},{9,1},... | collective-permute-start | bytes 393224 | tf_op jit(solution)/shard_map/ppermute | solution.py:263
  36.9 2.3 %collective-permute-start.13 = (bf16[8,8192]{1,0:T(8,128)(2,1)S(1)}, bf16[8,8192]{1,0:T(8,128)(2,1)S(1)}, u32[]{:S(2)}, u32[]{:S(2)}) collective-permute-start(bf16[8,8192]{1,0:T(8,128)(2,1)S(1)} %get-tuple-element.70), channel_id=1, source_target_pairs={{0,14},{1,13},{2,12},{3,15},{4,10},{5,9},{6,8},{7,11},{8,6},{9,5},... | collective-permute-start | bytes 393224 | tf_op jit(solution)/shard_map/ppermute | solution.py:263
  39.2 0.0 collective-permute-start.12
  39.2 0.7 %collective-permute-start.11 = (bf16[8,8192]{1,0:T(8,128)(2,1)S(1)}, bf16[8,8192]{1,0:T(8,128)(2,1)S(1)}, u32[]{:S(2)}, u32[]{:S(2)}) collective-permute-start(bf16[8,8192]{1,0:T(8,128)(2,1)S(1)} %get-tuple-element.72), channel_id=1, source_target_pairs={{0,0},{1,3},{2,2},{3,1},{4,4},{5,7},{6,6},{7,5},{8,8},{9,11},{10,1... | collective-permute-start | bytes 393224 | tf_op jit(solution)/shard_map/ppermute | solution.py:263
  39.8 9.1 %grads.1 = (bf16[4096,1024]{1,0:T(8,128)(2,1)}, bf16[4096,1024]{1,0:T(8,128)(2,1)}, bf16[1024,4096]{1,0:T(8,128)(2,1)}) custom-call(bf16[64,4096]{1,0:T(8,128)(2,1)S(1)} %get-tuple-element.53.tokens_ref, bf16[64,4096]{1,0:T(8,128)(2,1)S(1)} %get-tuple-element.54.cotangents_ref, bf16[64,1024]{1,0:T(8,128)(2,1)S(1)} %get-tuple-element.55.gate_delta_ref, ...), custom_call_target="tpu_custom_call" | custom-call | flops 1610612736 | bytes 25165824 | tf_op jit(solution)/shard_map/grads/pallas_call | solution.py:225
  49.0 0.0 collective-permute-done.14
  49.0 0.0 collective-permute-done.13
  49.0 0.0 collective-permute-done.12
  49.0 0.0 collective-permute-done.11
  49.0 0.1 convert_add_fusion
  49.1 0.4 collective-permute-start.15
  49.5 1.0 %collective-permute-done.15 = f32[4,8192]{1,0:T(4,128)S(1)} collective-permute-done((f32[4,8192]{1,0:T(4,128)S(1)}, f32[4,8192]{1,0:T(4,128)S(1)}, u32[]{:S(2)}, u32[]{:S(2)}) %collective-permute-start.15) | collective-permute-done | bytes 131104 | tf_op jit(solution)/shard_map/ppermute | solution.py:267
  50.6 0.7 %fusion.2 = (bf16[4,4096]{1,0:T(4,128)(2,1)}, bf16[4,4096]{1,0:T(4,128)(2,1)}) fusion(bf16[4,8192]{1,0:T(4,128)(2,1)S(1)} %fusion), kind=kLoop, calls=%fused_computation.8 | loop fusion | bytes 131072 | tf_op jit(solution)/shard_map/slice | solution.py:289
  (4 shorter events, 0.1 us)
Async XLA Ops:
  0.6 2.2 %collective-permute-start = (bf16[4,4096]{1,0:T(4,128)(2,1)}, bf16[4,4096]{1,0:T(4,128)(2,1)S(1)}, u32[]{:S(2)}, u32[]{:S(2)}) collective-permute-start(bf16[4,4096]{1,0:T(4,128)(2,1)} %param.6), channel_id=1, source_target_pairs={{0,1},{1,0},{2,3},{3,2},{4,5},{5,4},{6,7},{7,6},{8,9},{9,8},{10,11... | collective-permute-start | bytes 98312 | tf_op jit(solution)/shard_map/ppermute | solution.py:275
  1.1 1.6 %collective-permute-start.1 = (bf16[4,4096]{1,0:T(4,128)(2,1)}, bf16[4,4096]{1,0:T(4,128)(2,1)S(1)}, u32[]{:S(2)}, u32[]{:S(2)}) collective-permute-start(bf16[4,4096]{1,0:T(4,128)(2,1)} %param.7), channel_id=1, source_target_pairs={{0,1},{1,0},{2,3},{3,2},{4,5},{5,4},{6,7},{7,6},{8,9},{9,8},{10,11... | collective-permute-start | bytes 98312 | tf_op jit(solution)/shard_map/ppermute | solution.py:275
  2.9 16.3 %collective-permute-start.5 = (bf16[16,4096]{1,0:T(8,128)(2,1)S(1)}, bf16[16,4096]{1,0:T(8,128)(2,1)S(1)}, u32[]{:S(2)}, u32[]{:S(2)}) collective-permute-start(bf16[16,4096]{1,0:T(8,128)(2,1)S(1)} %pad_maximum_fusion.after_ref), channel_id=1, source_target_pairs={{0,10},{1,9},{2,8},{3,11},{4,14},{5,13},{6,12},{7,15},{8,2},{9,1},... | collective-permute-start | bytes 393224 | tf_op jit(solution)/shard_map/ppermute | solution.py:255
  8.0 11.2 %collective-permute-start.4 = (bf16[16,4096]{1,0:T(8,128)(2,1)S(1)}, bf16[16,4096]{1,0:T(8,128)(2,1)S(1)}, u32[]{:S(2)}, u32[]{:S(2)}) collective-permute-start(bf16[16,4096]{1,0:T(8,128)(2,1)S(1)} %pad_maximum_fusion.after_ref), channel_id=1, source_target_pairs={{0,14},{1,13},{2,12},{3,15},{4,10},{5,9},{6,8},{7,11},{8,6},{9,5},... | collective-permute-start | bytes 393224 | tf_op jit(solution)/shard_map/ppermute | solution.py:255
  9.2 9.9 %collective-permute-start.3 = (bf16[16,4096]{1,0:T(8,128)(2,1)S(1)}, bf16[16,4096]{1,0:T(8,128)(2,1)S(1)}, u32[]{:S(2)}, u32[]{:S(2)}) collective-permute-start(bf16[16,4096]{1,0:T(8,128)(2,1)S(1)} %pad_maximum_fusion.after_ref), channel_id=1, source_target_pairs={{0,6},{1,5},{2,4},{3,7},{4,2},{5,1},{6,0},{7,3},{8,14},{9,13},{10,... | collective-permute-start | bytes 393224 | tf_op jit(solution)/shard_map/ppermute | solution.py:255
  9.8 9.5 %collective-permute-start.2 = (bf16[16,4096]{1,0:T(8,128)(2,1)S(1)}, bf16[16,4096]{1,0:T(8,128)(2,1)S(1)}, u32[]{:S(2)}, u32[]{:S(2)}) collective-permute-start(bf16[16,4096]{1,0:T(8,128)(2,1)S(1)} %pad_maximum_fusion.after_ref), channel_id=1, source_target_pairs={{0,0},{1,3},{2,2},{3,1},{4,4},{5,7},{6,6},{7,5},{8,8},{9,11},{10,1... | collective-permute-start | bytes 393224 | tf_op jit(solution)/shard_map/ppermute | solution.py:255
  19.2 1.9 %collective-permute-start.6 = (bf16[16,4096]{1,0:T(8,128)(2,1)S(1)}, bf16[16,4096]{1,0:T(8,128)(2,1)S(1)}, u32[]{:S(2)}, u32[]{:S(2)}) collective-permute-start(bf16[16,4096]{1,0:T(8,128)(2,1)S(1)} %collective-permute-done.2.refs_0_), channel_id=1, source_target_pairs={{0,1},{1,0},{2,3},{3,2},{4,5},{5,4},{6,7},{7,6},{8,9},{9,8},{10,11... | collective-permute-start | bytes 393224 | tf_op jit(solution)/shard_map/ppermute | solution.py:257
  20.1 1.3 %collective-permute-start.7 = (bf16[16,4096]{1,0:T(8,128)(2,1)S(1)}, bf16[16,4096]{1,0:T(8,128)(2,1)S(1)}, u32[]{:S(2)}, u32[]{:S(2)}) collective-permute-start(bf16[16,4096]{1,0:T(8,128)(2,1)S(1)} %collective-permute-done.3.refs_1_), channel_id=1, source_target_pairs={{0,1},{1,0},{2,3},{3,2},{4,5},{5,4},{6,7},{7,6},{8,9},{9,8},{10,11... | collective-permute-start | bytes 393224 | tf_op jit(solution)/shard_map/ppermute | solution.py:257
  20.2 1.5 %collective-permute-start.8 = (bf16[16,4096]{1,0:T(8,128)(2,1)S(1)}, bf16[16,4096]{1,0:T(8,128)(2,1)S(1)}, u32[]{:S(2)}, u32[]{:S(2)}) collective-permute-start(bf16[16,4096]{1,0:T(8,128)(2,1)S(1)} %collective-permute-done.4.refs_2_), channel_id=1, source_target_pairs={{0,1},{1,0},{2,3},{3,2},{4,5},{5,4},{6,7},{7,6},{8,9},{9,8},{10,11... | collective-permute-start | bytes 393224 | tf_op jit(solution)/shard_map/ppermute | solution.py:257
  20.6 1.3 %collective-permute-start.9 = (bf16[16,4096]{1,0:T(8,128)(2,1)S(1)}, bf16[16,4096]{1,0:T(8,128)(2,1)S(1)}, u32[]{:S(2)}, u32[]{:S(2)}) collective-permute-start(bf16[16,4096]{1,0:T(8,128)(2,1)S(1)} %collective-permute-done.5.refs_3_), channel_id=1, source_target_pairs={{0,1},{1,0},{2,3},{3,2},{4,5},{5,4},{6,7},{7,6},{8,9},{9,8},{10,11... | collective-permute-start | bytes 393224 | tf_op jit(solution)/shard_map/ppermute | solution.py:257
  31.8 2.0 %collective-permute-start.10 = (bf16[32,8192]{1,0:T(8,128)(2,1)S(1)}, bf16[32,8192]{1,0:T(8,128)(2,1)S(1)}, u32[]{:S(2)}, u32[]{:S(2)}) collective-permute-start(bf16[32,8192]{1,0:T(8,128)(2,1)S(1)} %get-tuple-element.52), channel_id=1, source_target_pairs={{0,1},{1,0},{2,3},{3,2},{4,5},{5,4},{6,7},{7,6},{8,9},{9,8},{10,11... | collective-permute-start | bytes 1572872 | tf_op jit(solution)/shard_map/ppermute | solution.py:284
  34.0 15.0 %collective-permute-start.14 = (bf16[8,8192]{1,0:T(8,128)(2,1)S(1)}, bf16[8,8192]{1,0:T(8,128)(2,1)S(1)}, u32[]{:S(2)}, u32[]{:S(2)}) collective-permute-start(bf16[8,8192]{1,0:T(8,128)(2,1)S(1)} %get-tuple-element.69), channel_id=1, source_target_pairs={{0,10},{1,9},{2,8},{3,11},{4,14},{5,13},{6,12},{7,15},{8,2},{9,1},... | collective-permute-start | bytes 393224 | tf_op jit(solution)/shard_map/ppermute | solution.py:263
  36.9 12.1 %collective-permute-start.13 = (bf16[8,8192]{1,0:T(8,128)(2,1)S(1)}, bf16[8,8192]{1,0:T(8,128)(2,1)S(1)}, u32[]{:S(2)}, u32[]{:S(2)}) collective-permute-start(bf16[8,8192]{1,0:T(8,128)(2,1)S(1)} %get-tuple-element.70), channel_id=1, source_target_pairs={{0,14},{1,13},{2,12},{3,15},{4,10},{5,9},{6,8},{7,11},{8,6},{9,5},... | collective-permute-start | bytes 393224 | tf_op jit(solution)/shard_map/ppermute | solution.py:263
  39.2 9.8 %collective-permute-start.12 = (bf16[8,8192]{1,0:T(8,128)(2,1)S(1)}, bf16[8,8192]{1,0:T(8,128)(2,1)S(1)}, u32[]{:S(2)}, u32[]{:S(2)}) collective-permute-start(bf16[8,8192]{1,0:T(8,128)(2,1)S(1)} %get-tuple-element.71), channel_id=1, source_target_pairs={{0,6},{1,5},{2,4},{3,7},{4,2},{5,1},{6,0},{7,3},{8,14},{9,13},{10,... | collective-permute-start | bytes 393224 | tf_op jit(solution)/shard_map/ppermute | solution.py:263
  39.2 9.8 %collective-permute-start.11 = (bf16[8,8192]{1,0:T(8,128)(2,1)S(1)}, bf16[8,8192]{1,0:T(8,128)(2,1)S(1)}, u32[]{:S(2)}, u32[]{:S(2)}) collective-permute-start(bf16[8,8192]{1,0:T(8,128)(2,1)S(1)} %get-tuple-element.72), channel_id=1, source_target_pairs={{0,0},{1,3},{2,2},{3,1},{4,4},{5,7},{6,6},{7,5},{8,8},{9,11},{10,1... | collective-permute-start | bytes 393224 | tf_op jit(solution)/shard_map/ppermute | solution.py:263
  49.1 1.4 %collective-permute-start.15 = (f32[4,8192]{1,0:T(4,128)S(1)}, f32[4,8192]{1,0:T(4,128)S(1)}, u32[]{:S(2)}, u32[]{:S(2)}) collective-permute-start(f32[4,8192]{1,0:T(4,128)S(1)} %slice.45), channel_id=1, source_target_pairs={{0,1},{1,0},{2,3},{3,2},{4,5},{5,4},{6,7},{7,6},{8,9},{9,8},{10,11... | collective-permute-start | bytes 393224 | tf_op jit(solution)/shard_map/ppermute | solution.py:267

commit v5 on v4

--- a/solution.py
+++ b/solution.py
@@ -9,7 +9,7 @@
 
 AXIS = "tensor"
 BLOCK = 64
-CHUNKS = 8
+CHUNKS = 4
 PARTS = 8
 SLOTS = 10
 BF16 = jnp.bfloat16
@@ -134,14 +134,14 @@
         gate_delta_ref[:, at] = (hidden_grad * up * sig * (1.0 + gate * (1.0 - sig))).astype(BF16)
         up_delta_ref[:, at] = (hidden_grad * act).astype(BF16)
     half = tokens_ref.shape[0] // 2
-    for start in range(0, features, 512):
-        at = pl.ds(start, 512)
+    for start in range(0, features, 1024):
+        at = pl.ds(start, 1024)
         mixed = dot(hidden_ref[...], down_ref[:, at])
         mine_ref[:, at] = mixed[:half]
         theirs_ref[:, at] = mixed[half:].astype(BF16)
         grad = dot(gate_delta_ref[...], gate_t_ref[:, at])
         grad += dot(up_delta_ref[...], up_t_ref[:, at])
-        at = pl.ds(features + start, 512)
+        at = pl.ds(features + start, 1024)
         mine_ref[:, at] = grad[:half]
         theirs_ref[:, at] = grad[half:].astype(BF16)
 

time: 51.5 us -> 51 us (level)
  no operation moved by 1% of the time
where the time goes in v5:
time: 51 us; the launch traced here: 50.8 us
  Pallas kernels  27.3 us (54%)
  starting transfers between devices  16 us (31%)
  waiting for transfers between devices  4.03 us (8%)
  other arithmetic  1.87 us (4%)
  between operations  0.79 us (2%)
  local copies, waits for them, and re-layouts  0.74 us (1%)
    pallas_call x1, Pallas kernels, layer(): pl.pallas_call(functools.partial(layer_kernel, len(pieces)), out_shape=(s...  9.56 us
    pallas_call x1, Pallas kernels, grads(): pl.pallas_call(grads_kernel, out_shape=tuple((shape(*dims, dtype=BF16) fo...  9.12 us
    pallas_call x1, Pallas kernels, mask_weights(): pl.pallas_call(mask_kernel, out_shape=tuple((pltpu.VMEM(w.shape, BF16) fo...  8.61 us
    ppermute x4, starting transfers between devices, gather(): mine = [lax.ppermute(own, AXIS, pairs) for pairs in across_chips(devices)]  7.49 us
    ppermute x4, starting transfers between devices, scatter(): lax.ppermute(total[k * rows:(k + 1) * rows], AXIS, pairs)  5.82 us
    ppermute x1, waiting for transfers between devices, shards(): total = (mine + lax.ppermute(theirs, AXIS, cores).astype(F32)).astype(BF16)  1.72 us
    ppermute x4, starting transfers between devices, gather(): lax.ppermute(piece, AXIS, across_cores(devices))  1.48 us
    ppermute x4, waiting for transfers between devices, gather(): lax.ppermute(piece, AXIS, across_cores(devices))  1.27 us
  transfers between devices with their start and end apart: 16, of which 6 were waited for; matrix products, arithmetic and copies ran while one was open for 3% of the time, Pallas kernels for 35%

profile of v5, /device:TPU:0, one launch (start us, length us, event | category | flops | bytes accessed | tf_op | source)
XLA Modules:
  0.0 50.8 jit_solution(14766401488446117233)
XLA Ops:
  0.6 0.5 %collective-permute-start = (bf16[4,4096]{1,0:T(4,128)(2,1)}, bf16[4,4096]{1,0:T(4,128)(2,1)S(1)}, u32[]{:S(2)}, u32[]{:S(2)}) collective-permute-start(bf16[4,4096]{1,0:T(4,128)(2,1)} %param.6), channel_id=1, source_target_pairs={{0,1},{1,0},{2,3},{3,2},{4,5},{5,4},{6,7},{7,6},{8,9},{9,8},{10,11... | collective-permute-start | bytes 98312 | tf_op jit(solution)/shard_map/ppermute | solution.py:275
  1.1 0.1 collective-permute-start.1
  1.2 0.8 %pad_maximum_fusion.1 = bf16[8,4096]{1,0:T(8,128)(2,1)S(1)} fusion(bf16[4,4096]{1,0:T(4,128)(2,1)} %param.7, bf16[4,4096]{1,0:T(4,128)(2,1)} %param.6), kind=kLoop, calls=%fused_computation.5 | loop fusion | flops 131072 | bytes 131072 | tf_op jit(solution)/shard_map/concatenate | solution.py:273
  2.0 0.7 %convert_bitcast_fusion.flags_ref = bf16[3,16,64]{2,1,0:T(8,128)(2,1)S(1)} fusion(s32[3,64,16]{1,2,0:T(8,128)} %param.11), kind=kLoop, calls=%fused_computation.6 | loop fusion | flops 3072 | bytes 18432 | tf_op jit(solution)/shard_map/convert_element_type | solution.py:274
  2.8 0.0 collective-permute-done
  2.8 0.0 collective-permute-done.1
  2.8 0.1 pad_maximum_fusion.after_ref
  2.9 5.0 %collective-permute-start.5 = (bf16[16,4096]{1,0:T(8,128)(2,1)S(1)}, bf16[16,4096]{1,0:T(8,128)(2,1)S(1)}, u32[]{:S(2)}, u32[]{:S(2)}) collective-permute-start(bf16[16,4096]{1,0:T(8,128)(2,1)S(1)} %pad_maximum_fusion.after_ref), channel_id=1, source_target_pairs={{0,10},{1,9},{2,8},{3,11},{4,14},{5,13},{6,12},{7,15},{8,2},{9,1},... | collective-permute-start | bytes 393224 | tf_op jit(solution)/shard_map/ppermute | solution.py:255
  8.0 1.3 %collective-permute-start.4 = (bf16[16,4096]{1,0:T(8,128)(2,1)S(1)}, bf16[16,4096]{1,0:T(8,128)(2,1)S(1)}, u32[]{:S(2)}, u32[]{:S(2)}) collective-permute-start(bf16[16,4096]{1,0:T(8,128)(2,1)S(1)} %pad_maximum_fusion.after_ref), channel_id=1, source_target_pairs={{0,14},{1,13},{2,12},{3,15},{4,10},{5,9},{6,8},{7,11},{8,6},{9,5},... | collective-permute-start | bytes 393224 | tf_op jit(solution)/shard_map/ppermute | solution.py:255
  9.2 0.5 collective-permute-start.3
  9.8 0.7 %collective-permute-start.2 = (bf16[16,4096]{1,0:T(8,128)(2,1)S(1)}, bf16[16,4096]{1,0:T(8,128)(2,1)S(1)}, u32[]{:S(2)}, u32[]{:S(2)}) collective-permute-start(bf16[16,4096]{1,0:T(8,128)(2,1)S(1)} %pad_maximum_fusion.after_ref), channel_id=1, source_target_pairs={{0,0},{1,3},{2,2},{3,1},{4,4},{5,7},{6,6},{7,5},{8,8},{9,11},{10,1... | collective-permute-start | bytes 393224 | tf_op jit(solution)/shard_map/ppermute | solution.py:255
  10.4 8.6 %mask.1 = (bf16[4096,1024]{1,0:T(8,128)(2,1)S(1)}, bf16[4096,1024]{1,0:T(8,128)(2,1)S(1)}, bf16[1024,4096]{1,0:T(8,128)(2,1)S(1)}, bf16[1024,4096]{1,0:T(8,128)(...) custom-call(bf16[3,16,64]{2,1,0:T(8,128)(2,1)S(1)} %convert_bitcast_, ...), custom_call_target="tpu_custom_call" | custom-call | bytes 25165824 | tf_op jit(solution)/shard_map/mask/pallas_call | solution.py:99
  19.0 0.0 collective-permute-done.5.refs_3_
  19.1 0.0 collective-permute-done.4.refs_2_
  19.1 0.0 collective-permute-done.3.refs_1_
  19.1 0.0 collective-permute-done.2.refs_0_
  19.1 0.9 %collective-permute-start.6 = (bf16[16,4096]{1,0:T(8,128)(2,1)S(1)}, bf16[16,4096]{1,0:T(8,128)(2,1)S(1)}, u32[]{:S(2)}, u32[]{:S(2)}) collective-permute-start(bf16[16,4096]{1,0:T(8,128)(2,1)S(1)} %collective-permute-done.2.refs_0_), channel_id=1, source_target_pairs={{0,1},{1,0},{2,3},{3,2},{4,5},{5,4},{6,7},{7,6},{8,9},{9,8},{10,11... | collective-permute-start | bytes 393224 | tf_op jit(solution)/shard_map/ppermute | solution.py:257
  20.0 0.1 collective-permute-start.7
  20.0 0.4 collective-permute-start.8
  20.5 0.1 collective-permute-start.9
  20.6 0.4 collective-permute-done.6.refs_4_
  21.0 0.4 collective-permute-done.7.refs_5_
  21.3 0.2 collective-permute-done.8.refs_6_
  21.5 0.3 collective-permute-done.9.refs_7_
  21.8 9.6 %layer.1 = (bf16[64,4096]{1,0:T(8,128)(2,1)S(1)}, bf16[64,4096]{1,0:T(8,128)(2,1)S(1)}, bf16[64,1024]{1,0:T(8,128)(2,1)S(1)}, bf16[64,1024]{1,0:T(8,128)(2,1)S(1...) custom-call(bf16[16,4096]{1,0:T(8,128)(2,1)S(1)} %collective-permute-done.2.refs_0_, ...), custom_call_target="tpu_custom_call" | custom-call | flops 3221225472 | bytes 25165824 | tf_op jit(solution)/shard_map/layer/pallas_call | solution.py:152
  31.4 0.3 collective-permute-start.10
  31.7 1.7 %collective-permute-done.10 = bf16[32,8192]{1,0:T(8,128)(2,1)S(1)} collective-permute-done((bf16[32,8192]{1,0:T(8,128)(2,1)S(1)}, bf16[32,8192]{1,0:T(8,128)(2,1)S(1)}, u32[]{:S(2)}, u32[]{:S(2)}) %collective-permute-start.10) | collective-permute-done | bytes 524320 | tf_op jit(solution)/shard_map/ppermute | solution.py:284
  33.4 0.1 add_convert_fusion.after_ref
  33.6 3.0 %collective-permute-start.14 = (bf16[8,8192]{1,0:T(8,128)(2,1)S(1)}, bf16[8,8192]{1,0:T(8,128)(2,1)S(1)}, u32[]{:S(2)}, u32[]{:S(2)}) collective-permute-start(bf16[8,8192]{1,0:T(8,128)(2,1)S(1)} %get-tuple-element.69), channel_id=1, source_target_pairs={{0,10},{1,9},{2,8},{3,11},{4,14},{5,13},{6,12},{7,15},{8,2},{9,1},... | collective-permute-start | bytes 393224 | tf_op jit(solution)/shard_map/ppermute | solution.py:263
  36.5 2.2 %collective-permute-start.13 = (bf16[8,8192]{1,0:T(8,128)(2,1)S(1)}, bf16[8,8192]{1,0:T(8,128)(2,1)S(1)}, u32[]{:S(2)}, u32[]{:S(2)}) collective-permute-start(bf16[8,8192]{1,0:T(8,128)(2,1)S(1)} %get-tuple-element.70), channel_id=1, source_target_pairs={{0,14},{1,13},{2,12},{3,15},{4,10},{5,9},{6,8},{7,11},{8,6},{9,5},... | collective-permute-start | bytes 393224 | tf_op jit(solution)/shard_map/ppermute | solution.py:263
  38.7 0.0 collective-permute-start.12
  38.7 0.7 %collective-permute-start.11 = (bf16[8,8192]{1,0:T(8,128)(2,1)S(1)}, bf16[8,8192]{1,0:T(8,128)(2,1)S(1)}, u32[]{:S(2)}, u32[]{:S(2)}) collective-permute-start(bf16[8,8192]{1,0:T(8,128)(2,1)S(1)} %get-tuple-element.72), channel_id=1, source_target_pairs={{0,0},{1,3},{2,2},{3,1},{4,4},{5,7},{6,6},{7,5},{8,8},{9,11},{10,1... | collective-permute-start | bytes 393224 | tf_op jit(solution)/shard_map/ppermute | solution.py:263
  39.4 9.1 %grads.1 = (bf16[4096,1024]{1,0:T(8,128)(2,1)}, bf16[4096,1024]{1,0:T(8,128)(2,1)}, bf16[1024,4096]{1,0:T(8,128)(2,1)}) custom-call(bf16[64,4096]{1,0:T(8,128)(2,1)S(1)} %get-tuple-element.53.tokens_ref, bf16[64,4096]{1,0:T(8,128)(2,1)S(1)} %get-tuple-element.54.cotangents_ref, bf16[64,1024]{1,0:T(8,128)(2,1)S(1)} %get-tuple-element.55.gate_delta_ref, ...), custom_call_target="tpu_custom_call" | custom-call | flops 1610612736 | bytes 25165824 | tf_op jit(solution)/shard_map/grads/pallas_call | solution.py:225
  48.5 0.0 collective-permute-done.14
  48.5 0.0 collective-permute-done.13
  48.5 0.0 collective-permute-done.12
  48.5 0.0 collective-permute-done.11
  48.6 0.1 convert_add_fusion
  48.7 0.4 collective-permute-start.15
  49.1 1.0 %collective-permute-done.15 = f32[4,8192]{1,0:T(4,128)S(1)} collective-permute-done((f32[4,8192]{1,0:T(4,128)S(1)}, f32[4,8192]{1,0:T(4,128)S(1)}, u32[]{:S(2)}, u32[]{:S(2)}) %collective-permute-start.15) | collective-permute-done | bytes 131104 | tf_op jit(solution)/shard_map/ppermute | solution.py:267
  50.1 0.7 %fusion.2 = (bf16[4,4096]{1,0:T(4,128)(2,1)}, bf16[4,4096]{1,0:T(4,128)(2,1)}) fusion(bf16[4,8192]{1,0:T(4,128)(2,1)S(1)} %fusion), kind=kLoop, calls=%fused_computation.8 | loop fusion | bytes 131072 | tf_op jit(solution)/shard_map/slice | solution.py:289
  (4 shorter events, 0.1 us)
Async XLA Ops:
  0.6 2.2 %collective-permute-start = (bf16[4,4096]{1,0:T(4,128)(2,1)}, bf16[4,4096]{1,0:T(4,128)(2,1)S(1)}, u32[]{:S(2)}, u32[]{:S(2)}) collective-permute-start(bf16[4,4096]{1,0:T(4,128)(2,1)} %param.6), channel_id=1, source_target_pairs={{0,1},{1,0},{2,3},{3,2},{4,5},{5,4},{6,7},{7,6},{8,9},{9,8},{10,11... | collective-permute-start | bytes 98312 | tf_op jit(solution)/shard_map/ppermute | solution.py:275
  1.1 1.6 %collective-permute-start.1 = (bf16[4,4096]{1,0:T(4,128)(2,1)}, bf16[4,4096]{1,0:T(4,128)(2,1)S(1)}, u32[]{:S(2)}, u32[]{:S(2)}) collective-permute-start(bf16[4,4096]{1,0:T(4,128)(2,1)} %param.7), channel_id=1, source_target_pairs={{0,1},{1,0},{2,3},{3,2},{4,5},{5,4},{6,7},{7,6},{8,9},{9,8},{10,11... | collective-permute-start | bytes 98312 | tf_op jit(solution)/shard_map/ppermute | solution.py:275
  2.9 16.1 %collective-permute-start.5 = (bf16[16,4096]{1,0:T(8,128)(2,1)S(1)}, bf16[16,4096]{1,0:T(8,128)(2,1)S(1)}, u32[]{:S(2)}, u32[]{:S(2)}) collective-permute-start(bf16[16,4096]{1,0:T(8,128)(2,1)S(1)} %pad_maximum_fusion.after_ref), channel_id=1, source_target_pairs={{0,10},{1,9},{2,8},{3,11},{4,14},{5,13},{6,12},{7,15},{8,2},{9,1},... | collective-permute-start | bytes 393224 | tf_op jit(solution)/shard_map/ppermute | solution.py:255
  8.0 11.1 %collective-permute-start.4 = (bf16[16,4096]{1,0:T(8,128)(2,1)S(1)}, bf16[16,4096]{1,0:T(8,128)(2,1)S(1)}, u32[]{:S(2)}, u32[]{:S(2)}) collective-permute-start(bf16[16,4096]{1,0:T(8,128)(2,1)S(1)} %pad_maximum_fusion.after_ref), channel_id=1, source_target_pairs={{0,14},{1,13},{2,12},{3,15},{4,10},{5,9},{6,8},{7,11},{8,6},{9,5},... | collective-permute-start | bytes 393224 | tf_op jit(solution)/shard_map/ppermute | solution.py:255
  9.2 9.8 %collective-permute-start.3 = (bf16[16,4096]{1,0:T(8,128)(2,1)S(1)}, bf16[16,4096]{1,0:T(8,128)(2,1)S(1)}, u32[]{:S(2)}, u32[]{:S(2)}) collective-permute-start(bf16[16,4096]{1,0:T(8,128)(2,1)S(1)} %pad_maximum_fusion.after_ref), channel_id=1, source_target_pairs={{0,6},{1,5},{2,4},{3,7},{4,2},{5,1},{6,0},{7,3},{8,14},{9,13},{10,... | collective-permute-start | bytes 393224 | tf_op jit(solution)/shard_map/ppermute | solution.py:255
  9.8 9.3 %collective-permute-start.2 = (bf16[16,4096]{1,0:T(8,128)(2,1)S(1)}, bf16[16,4096]{1,0:T(8,128)(2,1)S(1)}, u32[]{:S(2)}, u32[]{:S(2)}) collective-permute-start(bf16[16,4096]{1,0:T(8,128)(2,1)S(1)} %pad_maximum_fusion.after_ref), channel_id=1, source_target_pairs={{0,0},{1,3},{2,2},{3,1},{4,4},{5,7},{6,6},{7,5},{8,8},{9,11},{10,1... | collective-permute-start | bytes 393224 | tf_op jit(solution)/shard_map/ppermute | solution.py:255
  19.1 1.9 %collective-permute-start.6 = (bf16[16,4096]{1,0:T(8,128)(2,1)S(1)}, bf16[16,4096]{1,0:T(8,128)(2,1)S(1)}, u32[]{:S(2)}, u32[]{:S(2)}) collective-permute-start(bf16[16,4096]{1,0:T(8,128)(2,1)S(1)} %collective-permute-done.2.refs_0_), channel_id=1, source_target_pairs={{0,1},{1,0},{2,3},{3,2},{4,5},{5,4},{6,7},{7,6},{8,9},{9,8},{10,11... | collective-permute-start | bytes 393224 | tf_op jit(solution)/shard_map/ppermute | solution.py:257
  20.0 1.3 %collective-permute-start.7 = (bf16[16,4096]{1,0:T(8,128)(2,1)S(1)}, bf16[16,4096]{1,0:T(8,128)(2,1)S(1)}, u32[]{:S(2)}, u32[]{:S(2)}) collective-permute-start(bf16[16,4096]{1,0:T(8,128)(2,1)S(1)} %collective-permute-done.3.refs_1_), channel_id=1, source_target_pairs={{0,1},{1,0},{2,3},{3,2},{4,5},{5,4},{6,7},{7,6},{8,9},{9,8},{10,11... | collective-permute-start | bytes 393224 | tf_op jit(solution)/shard_map/ppermute | solution.py:257
  20.0 1.5 %collective-permute-start.8 = (bf16[16,4096]{1,0:T(8,128)(2,1)S(1)}, bf16[16,4096]{1,0:T(8,128)(2,1)S(1)}, u32[]{:S(2)}, u32[]{:S(2)}) collective-permute-start(bf16[16,4096]{1,0:T(8,128)(2,1)S(1)} %collective-permute-done.4.refs_2_), channel_id=1, source_target_pairs={{0,1},{1,0},{2,3},{3,2},{4,5},{5,4},{6,7},{7,6},{8,9},{9,8},{10,11... | collective-permute-start | bytes 393224 | tf_op jit(solution)/shard_map/ppermute | solution.py:257
  20.5 1.3 %collective-permute-start.9 = (bf16[16,4096]{1,0:T(8,128)(2,1)S(1)}, bf16[16,4096]{1,0:T(8,128)(2,1)S(1)}, u32[]{:S(2)}, u32[]{:S(2)}) collective-permute-start(bf16[16,4096]{1,0:T(8,128)(2,1)S(1)} %collective-permute-done.5.refs_3_), channel_id=1, source_target_pairs={{0,1},{1,0},{2,3},{3,2},{4,5},{5,4},{6,7},{7,6},{8,9},{9,8},{10,11... | collective-permute-start | bytes 393224 | tf_op jit(solution)/shard_map/ppermute | solution.py:257
  31.4 2.0 %collective-permute-start.10 = (bf16[32,8192]{1,0:T(8,128)(2,1)S(1)}, bf16[32,8192]{1,0:T(8,128)(2,1)S(1)}, u32[]{:S(2)}, u32[]{:S(2)}) collective-permute-start(bf16[32,8192]{1,0:T(8,128)(2,1)S(1)} %get-tuple-element.52), channel_id=1, source_target_pairs={{0,1},{1,0},{2,3},{3,2},{4,5},{5,4},{6,7},{7,6},{8,9},{9,8},{10,11... | collective-permute-start | bytes 1572872 | tf_op jit(solution)/shard_map/ppermute | solution.py:284
  33.6 15.0 %collective-permute-start.14 = (bf16[8,8192]{1,0:T(8,128)(2,1)S(1)}, bf16[8,8192]{1,0:T(8,128)(2,1)S(1)}, u32[]{:S(2)}, u32[]{:S(2)}) collective-permute-start(bf16[8,8192]{1,0:T(8,128)(2,1)S(1)} %get-tuple-element.69), channel_id=1, source_target_pairs={{0,10},{1,9},{2,8},{3,11},{4,14},{5,13},{6,12},{7,15},{8,2},{9,1},... | collective-permute-start | bytes 393224 | tf_op jit(solution)/shard_map/ppermute | solution.py:263
  36.5 12.0 %collective-permute-start.13 = (bf16[8,8192]{1,0:T(8,128)(2,1)S(1)}, bf16[8,8192]{1,0:T(8,128)(2,1)S(1)}, u32[]{:S(2)}, u32[]{:S(2)}) collective-permute-start(bf16[8,8192]{1,0:T(8,128)(2,1)S(1)} %get-tuple-element.70), channel_id=1, source_target_pairs={{0,14},{1,13},{2,12},{3,15},{4,10},{5,9},{6,8},{7,11},{8,6},{9,5},... | collective-permute-start | bytes 393224 | tf_op jit(solution)/shard_map/ppermute | solution.py:263
  38.7 9.8 %collective-permute-start.12 = (bf16[8,8192]{1,0:T(8,128)(2,1)S(1)}, bf16[8,8192]{1,0:T(8,128)(2,1)S(1)}, u32[]{:S(2)}, u32[]{:S(2)}) collective-permute-start(bf16[8,8192]{1,0:T(8,128)(2,1)S(1)} %get-tuple-element.71), channel_id=1, source_target_pairs={{0,6},{1,5},{2,4},{3,7},{4,2},{5,1},{6,0},{7,3},{8,14},{9,13},{10,... | collective-permute-start | bytes 393224 | tf_op jit(solution)/shard_map/ppermute | solution.py:263
  38.7 9.8 %collective-permute-start.11 = (bf16[8,8192]{1,0:T(8,128)(2,1)S(1)}, bf16[8,8192]{1,0:T(8,128)(2,1)S(1)}, u32[]{:S(2)}, u32[]{:S(2)}) collective-permute-start(bf16[8,8192]{1,0:T(8,128)(2,1)S(1)} %get-tuple-element.72), channel_id=1, source_target_pairs={{0,0},{1,3},{2,2},{3,1},{4,4},{5,7},{6,6},{7,5},{8,8},{9,11},{10,1... | collective-permute-start | bytes 393224 | tf_op jit(solution)/shard_map/ppermute | solution.py:263
  48.7 1.4 %collective-permute-start.15 = (f32[4,8192]{1,0:T(4,128)S(1)}, f32[4,8192]{1,0:T(4,128)S(1)}, u32[]{:S(2)}, u32[]{:S(2)}) collective-permute-start(f32[4,8192]{1,0:T(4,128)S(1)} %slice.45), channel_id=1, source_target_pairs={{0,1},{1,0},{2,3},{3,2},{4,5},{5,4},{6,7},{7,6},{8,9},{9,8},{10,11... | collective-permute-start | bytes 393224 | tf_op jit(solution)/shard_map/ppermute | solution.py:267
